TPU v7x, 512 devices: a whole 4x4x16 slice. The times are simulated.
512 devices in a mesh: mode: 4 (over y_hi, core), space: 128 (over y_lo, z, x).
Axes of the slice: x: 4, y: 4 (y_hi: 2, y_lo: 2; y = y_hi * 2 + y_lo), z: 16, core: 2. Of those that a mesh axis runs over, the one named last changes fastest.
Arguments:
- modes: float32 [20, 4, 1024, 1024], P('mode', None, 'space'), may hold values from -6 to 6
- coefficients: float32 [4, 4, 1024, 1024], P(None, None, 'space'), may hold values from 0.3 to 3
- coupling: int32 [80, 3], replicated, may hold values from 0 to 19, as said below
- coupling_values: float32 [80], replicated, may hold values from -3 to 3, as said below
- assignment: int32 [20], replicated, may hold values from 0 to 19, each once
Outputs:
- product: float32 [20, 4, 1024, 1024], P('mode', None, 'space')
Inputs may be any that keep to these rules, and one draw needn't show every extreme that they name: `coupling`: each mode stands for a multi-index of total degree at most 3 in 3 variables (which mode is which varies). Entry e < 20 is (e, e, 0). The other entries are exactly the pairs (i, j, k) whose multi-indices differ by one in variable k (k of 1 to 3), each pair listed once in each order, in an order that varies. `coupling_values`: the entries (i, j, k) and (j, i, k) carry the same value.
All inputs are finite; a program needn't handle non-finite values.
Results may differ from a plain program's by a relative error of at most 0.0003.
Values sent between devices are 32-bit elements; how exact they have to be, the bound alone decides.
A program may use at most 64 MiB of HBM per device.

v0:
```python
import jax
import jax.numpy as jnp
from jax import lax
from jax.sharding import PartitionSpec as P


def padded(x, sides, width):
    for axis, dim in sides:
        size, length = (lax.axis_size(axis), x.shape[dim])
        up = [(i, (i + 1) % size) for i in range(size - 1)]
        down = [(j, i) for i, j in up]
        last = lax.slice_in_dim(x, length - width, length, axis=dim)
        initial = lax.slice_in_dim(x, 0, width, axis=dim)
        before = lax.ppermute(last, axis, up)
        after = lax.ppermute(initial, axis, down)
        x = jnp.concatenate([before, x, after], axis=dim)
    return x


def slot_tensor(coupling, coupling_values, assignment, modes_count, terms_count):
    width = jnp.arange(modes_count, dtype=jnp.int32)
    terms = jnp.arange(terms_count, dtype=jnp.int32)
    test_hot = (coupling[:, 0:1] == width[None, :]).astype(jnp.float32)
    trial_hot = (coupling[:, 1:2] == width[None, :]).astype(jnp.float32)
    term_hot = (coupling[:, 2:3] == terms[None, :]).astype(jnp.float32)
    dense = jnp.einsum(
        "e,ei,ej,ek->ijk",
        coupling_values,
        test_hot,
        trial_hot,
        term_hot,
        precision=lax.Precision.HIGHEST,
    )
    placed = (assignment[:, None] == width[None, :]).astype(jnp.float32)
    return jnp.einsum("ai,bj,ijk->abk", placed, placed, dense, precision=lax.Precision.HIGHEST)


def apply_terms(field_ext, coef_ext):
    lead = field_ext.ndim - 3
    widths = [(0, 0)] * lead + [(1, 1), (0, 0), (1, 1)]
    field_pad = jnp.pad(field_ext, widths)
    coef_pad = jnp.pad(coef_ext, [(0, 0), (1, 1), (0, 0), (1, 1)])
    plane_count = field_ext.shape[-3]
    row_count = field_ext.shape[-2] - 2
    col_count = field_ext.shape[-1]
    centre_field = field_pad[..., 1 : plane_count + 1, 1 : row_count + 1, 1 : col_count + 1]
    centre_coef = coef_pad[..., 1 : plane_count + 1, 1 : row_count + 1, 1 : col_count + 1]
    total = jnp.zeros_like(centre_coef * centre_field)
    for offset in ((1, 0, 0), (-1, 0, 0), (0, 1, 0), (0, -1, 0), (0, 0, 1), (0, 0, -1)):
        plane_at = 1 + offset[0]
        row_at = 1 + offset[1]
        col_at = 1 + offset[2]
        other_field = field_pad[
            ...,
            plane_at : plane_at + plane_count,
            row_at : row_at + row_count,
            col_at : col_at + col_count,
        ]
        other_coef = coef_pad[
            ...,
            plane_at : plane_at + plane_count,
            row_at : row_at + row_count,
            col_at : col_at + col_count,
        ]
        total = total + 0.5 * (centre_coef + other_coef) * (centre_field - other_field)
    return total


def shards(modes, coefficients, coupling, coupling_values, assignment):
    group_size = modes.shape[0]
    total_modes = assignment.shape[0]
    term_count = coefficients.shape[0]
    slots = slot_tensor(coupling, coupling_values, assignment, total_modes, term_count)
    first_slot = lax.axis_index("mode") * group_size
    coef_ext = padded(coefficients, (("space", 2),), 1)
    my_rows = lax.dynamic_slice_in_dim(slots, first_slot, group_size, 0)
    modes_ext = padded(modes, (("space", 2),), 1)
    terms = apply_terms(lax.all_gather(modes_ext, "mode", axis=0, tiled=True)[:, None], coef_ext)
    return jnp.einsum("ajk,jkpxy->apxy", my_rows, terms, precision=lax.Precision.HIGHEST)


def solution(mesh):
    in_specs = (P("mode", None, "space", None), P(None, None, "space", None), P(), P(), P())
    out_specs = P("mode", None, "space", None)
    return jax.shard_map(shards, mesh=mesh, in_specs=in_specs, out_specs=out_specs, check_vma=False)
```

profile of v0, /device:TPU:1, one launch (start us, length us, event | category | flops | bytes accessed | tf_op | source)
XLA Modules:
  0.0 109.2 jit_solution(17068849569659193618)
XLA Ops:
  6.6 1.5 %fusion.64 = (f32[5,4,1,1024]{3,2,1,0:T(1,128)S(1)}, f32[5,4,1,1024]{3,2,1,0:T(1,128)S(1)}) fusion(f32[5,4,8,1024]{3,2,1,0:T(8,128)} %param.5), kind=kLoop, calls=%fused_computation.87 | loop fusion | bytes 327680 | tf_op jit(solution)/shard_map/slice | solution.py:12
  8.1 4.0 %collective-permute-start.2 = (f32[5,4,1,1024]{3,0,2,1:T(8,128)S(1)}, f32[5,4,1,1024]{3,0,2,1:T(8,128)S(1)}, u32[]{:S(2)}, u32[]{:S(2)}) collective-permute-start(f32[5,4,1,1024]{3,0,2,1:T(8,128)S(1)} %copy.42), channel_id=1, source_target_pairs={{0,1},{1,2},{2,3},{3,4},{4,5},{5,6},{6,7},{7,8},{8,9},{9,10},{10,1... | collective-permute-start | bytes 245768 | tf_op jit(solution)/shard_map/ppermute | solution.py:14
  12.1 1.3 %collective-permute-start.3 = (f32[5,4,1,1024]{3,0,2,1:T(8,128)S(1)}, f32[5,4,1,1024]{3,0,2,1:T(8,128)S(1)}, u32[]{:S(2)}, u32[]{:S(2)}) collective-permute-start(f32[5,4,1,1024]{3,0,2,1:T(8,128)S(1)} %copy.43), channel_id=1, source_target_pairs={{1,0},{2,1},{3,2},{4,3},{5,4},{6,5},{7,6},{8,7},{9,8},{10,9},{11,1... | collective-permute-start | bytes 245768 | tf_op jit(solution)/shard_map/ppermute | solution.py:15
  13.4 1.5 %copy.23 = f32[5,4,8,1024]{3,1,2,0:T(4,128)S(1)} copy(f32[5,4,8,1024]{3,2,1,0:T(8,128)} %param.5) | data formatting | bytes 1310720 | tf_op args[0]
  15.0 2.8 %collective-permute-done.3 = f32[5,4,1,1024]{3,0,2,1:T(8,128)S(1)} collective-permute-done((f32[5,4,1,1024]{3,0,2,1:T(8,128)S(1)}, f32[5,4,1,1024]{3,0,2,1:T(8,128)S(1)}, u32[]{:S(2)}, u32[]{:S(2)}) %collective-permute-start.3) | collective-permute-done | bytes 81952 | tf_op jit(solution)/shard_map/ppermute | solution.py:15
  17.9 1.2 %pad_maximum_fusion = f32[5,4,10,1024]{3,1,2,0:T(4,128)} fusion(f32[5,4,1,1024]{3,1,2,0:T(4,128)S(1)} %copy.24, f32[5,4,8,1024]{3,1,2,0:T(4,128)S(1)} %copy.23, f32[5,4,1,1024]{3,1,2,0:T(4,128)S(1)} %copy.22), kind=kLoop, calls=%fused_computation.51 | loop fusion | flops 409600 | bytes 1638400 | tf_op jit(solution)/shard_map/concatenate | solution.py:16
  19.1 0.1 fusion.65
  19.2 3.4 %collective-permute-start = (f32[4,4,1,1024]{3,2,1,0:T(1,128)S(1)}, f32[4,4,1,1024]{3,2,1,0:T(1,128)S(1)}, u32[]{:S(2)}, u32[]{:S(2)}) collective-permute-start(f32[4,4,1,1024]{3,2,1,0:T(1,128)S(1)} %get-tuple-element.19), channel_id=1, source_target_pairs={{0,1},{1,2},{2,3},{3,4},{4,5},{5,6},{6,7},{7,8},{8,9},{9,10},{10,1... | collective-permute-start | bytes 196616 | tf_op jit(solution)/shard_map/ppermute | solution.py:14
  22.6 1.3 %collective-permute-start.1 = (f32[4,4,1,1024]{3,2,1,0:T(1,128)S(1)}, f32[4,4,1,1024]{3,2,1,0:T(1,128)S(1)}, u32[]{:S(2)}, u32[]{:S(2)}) collective-permute-start(f32[4,4,1,1024]{3,2,1,0:T(1,128)S(1)} %get-tuple-element.20), channel_id=1, source_target_pairs={{1,0},{2,1},{3,2},{4,3},{5,4},{6,5},{7,6},{8,7},{9,8},{10,9},{11,1... | collective-permute-start | bytes 196616 | tf_op jit(solution)/shard_map/ppermute | solution.py:15
  24.1 0.1 broadcast_multiply_fusion
  24.3 0.3 convolution_bitcast_fusion
  24.6 0.2 fusion.59
  24.9 0.2 fusion.57
  25.2 2.5 %collective-permute-done.1 = f32[4,4,1,1024]{3,2,1,0:T(1,128)S(1)} collective-permute-done((f32[4,4,1,1024]{3,2,1,0:T(1,128)S(1)}, f32[4,4,1,1024]{3,2,1,0:T(1,128)S(1)}, u32[]{:S(2)}, u32[]{:S(2)}) %collective-permute-start.1) | collective-permute-done | bytes 65568 | tf_op jit(solution)/shard_map/ppermute | solution.py:15
  27.7 0.7 select_maximum_fusion
  28.4 0.6 fusion.47
  28.9 0.3 copy.19
  29.3 0.3 copy.26
  29.6 0.3 copy.28
  30.0 0.3 copy.30
  30.3 0.3 copy.32
  30.7 0.3 copy.34
  31.0 37.6 %all-gather.2.cloned.1.call-done = f32[20,4,10,1024]{3,1,2,0:T(4,128)} async-done(((f32[5,4,10,1024]{3,1,2,0:T(4,128)}), f32[20,4,10,1024]{3,1,2,0:T(4,128)}) %all-gather.2.cloned.1.call-update) | async-done | bytes 3276816 | tf_op jit(solution)/shard_map/all_gather | solution.py:78
  68.6 10.6 %fusion.25 = (f32[20,4,8,1024]{3,1,2,0:T(4,128)S(1)}, f32[20,4,8,1024]{3,1,2,0:T(4,128)S(1)}, f32[20,4,8,1024]{3,1,2,0:T(4,128)S(1)}, f32[20,4,8,1024]{3,1,2,0:T...) fusion(f32[20,1,4,10,1024]{4,2,3,0,1:T(4,128)} %bitcast.40), kind=kLoop, calls=%fused_computation.33 | loop fusion | flops 3932160 | bytes 26869760 | tf_op jit(solution)/shard_map/mul | solution.py:65
  79.3 1.5 %copy.25 = f32[20,4,8,1024]{3,0,2,1:T(8,128)S(1)} copy(f32[20,4,8,1024]{3,1,2,0:T(4,128)S(1)} %get-tuple-element.5) | data formatting | bytes 5242880 | tf_op jit(solution)/shard_map/mul | solution.py:65
  80.8 1.5 %copy.27 = f32[20,4,8,1024]{3,0,2,1:T(8,128)S(1)} copy(f32[20,4,8,1024]{3,1,2,0:T(4,128)S(1)} %get-tuple-element.10) | data formatting | bytes 5242880 | tf_op jit(solution)/shard_map/mul | solution.py:65
  82.4 1.5 %copy.29 = f32[20,4,8,1024]{3,0,2,1:T(8,128)S(1)} copy(f32[20,4,8,1024]{3,1,2,0:T(4,128)S(1)} %get-tuple-element.9) | data formatting | bytes 5242880 | tf_op jit(solution)/shard_map/mul | solution.py:65
  83.9 1.5 %copy.31 = f32[20,4,8,1024]{3,0,2,1:T(8,128)S(1)} copy(f32[20,4,8,1024]{3,1,2,0:T(4,128)S(1)} %get-tuple-element.8) | data formatting | bytes 5242880 | tf_op jit(solution)/shard_map/mul | solution.py:65
  85.5 1.5 %copy.33 = f32[20,4,8,1024]{3,0,2,1:T(8,128)S(1)} copy(f32[20,4,8,1024]{3,1,2,0:T(4,128)S(1)} %get-tuple-element.6) | data formatting | bytes 5242880 | tf_op jit(solution)/shard_map/mul | solution.py:65
  87.0 1.5 %copy.35 = f32[20,4,8,1024]{3,0,2,1:T(8,128)S(1)} copy(f32[20,4,8,1024]{3,1,2,0:T(4,128)S(1)} %get-tuple-element.7) | data formatting | bytes 5242880 | tf_op jit(solution)/shard_map/mul | solution.py:65
  88.6 12.6 %fusion.37 = f32[5,4,8,1024]{3,0,2,1:T(8,128)S(1)} fusion(f32[20,4,8,1024]{3,0,2,1:T(8,128)S(1)} %copy.35, f32[4,4,8,1024]{3,0,2,1:T(4,128)S(1)} %copy.34, f32[20,4,8,1024]{3,0,2,1:T(8,128)S(1)} %copy.33, f32[4,4,8,1024]{3,0,2,1:T(4,128)S(1)} %copy.32, f32[20,4,8,1024]{3,0,2,1:T(8,128)S(1)} %copy.31, f32[4,4,8,1024]{3,0,2,1:T(4,128)S(1)} %copy.30, ...), kind=kOutput, calls=%fused_computation.49 | convolution fusion | flops 186122240 | bytes 22691844 | tf_op jit(solution)/shard_map/ajk,jkpxy->apxy/dot_general | solution.py:79
  101.2 1.2 %copy.36 = f32[5,4,8,1024]{3,2,1,0:T(8,128)} copy(f32[5,4,8,1024]{3,0,2,1:T(8,128)S(1)} %fusion.37) | data formatting | bytes 1310720 | tf_op jit(solution)/shard_map/ajk,jkpxy->apxy/dot_general | solution.py:79
  (19 shorter events, 0.5 us)
Async XLA Ops:
  6.5 12.6 %copy-start = (f32[4,4,8,1024]{3,2,1,0:T(8,128)S(1)}, f32[4,4,8,1024]{3,2,1,0:T(8,128)}, u32[]{:S(2)}) copy-start(f32[4,4,8,1024]{3,2,1,0:T(8,128)} %param.6) | copy-start | bytes 1572868
  6.5 17.4 %copy-start.2 = (s32[80,3]{0,1:T(4,128)S(1)}, s32[80,3]{0,1:T(4,128)}, u32[]{:S(2)}) copy-start(s32[80,3]{0,1:T(4,128)} %param.7) | copy-start | bytes 2884
  6.5 17.5 %copy-start.3 = (f32[80]{0:T(128)S(1)}, f32[80]{0:T(128)}, u32[]{:S(2)}) copy-start(f32[80]{0:T(128)} %param.8) | copy-start | bytes 964
  6.5 18.1 %copy-start.1 = (s32[20]{0:T(128)S(1)}, s32[20]{0:T(128)}, u32[]{:S(2)}) copy-start(s32[20]{0:T(128)} %param.9) | copy-start | bytes 244
  6.5 62.1 %all-gather.2.cloned.1.call-start = ((), (), s32[]{:S(2)}) async-start(), calls=%async_computation | async-start | bytes 4096000 | tf_op jit(solution)/shard_map/all_gather | solution.py:78
  8.1 6.8 %collective-permute-start.2 = (f32[5,4,1,1024]{3,0,2,1:T(8,128)S(1)}, f32[5,4,1,1024]{3,0,2,1:T(8,128)S(1)}, u32[]{:S(2)}, u32[]{:S(2)}) collective-permute-start(f32[5,4,1,1024]{3,0,2,1:T(8,128)S(1)} %copy.42), channel_id=1, source_target_pairs={{0,1},{1,2},{2,3},{3,4},{4,5},{5,6},{6,7},{7,8},{8,9},{9,10},{10,1... | collective-permute-start | bytes 245768 | tf_op jit(solution)/shard_map/ppermute | solution.py:14
  12.1 5.7 %collective-permute-start.3 = (f32[5,4,1,1024]{3,0,2,1:T(8,128)S(1)}, f32[5,4,1,1024]{3,0,2,1:T(8,128)S(1)}, u32[]{:S(2)}, u32[]{:S(2)}) collective-permute-start(f32[5,4,1,1024]{3,0,2,1:T(8,128)S(1)} %copy.43), channel_id=1, source_target_pairs={{1,0},{2,1},{3,2},{4,3},{5,4},{6,5},{7,6},{8,7},{9,8},{10,9},{11,1... | collective-permute-start | bytes 245768 | tf_op jit(solution)/shard_map/ppermute | solution.py:15
  19.2 5.9 %collective-permute-start = (f32[4,4,1,1024]{3,2,1,0:T(1,128)S(1)}, f32[4,4,1,1024]{3,2,1,0:T(1,128)S(1)}, u32[]{:S(2)}, u32[]{:S(2)}) collective-permute-start(f32[4,4,1,1024]{3,2,1,0:T(1,128)S(1)} %get-tuple-element.19), channel_id=1, source_target_pairs={{0,1},{1,2},{2,3},{3,4},{4,5},{5,6},{6,7},{7,8},{8,9},{9,10},{10,1... | collective-permute-start | bytes 196616 | tf_op jit(solution)/shard_map/ppermute | solution.py:14
  22.6 5.0 %collective-permute-start.1 = (f32[4,4,1,1024]{3,2,1,0:T(1,128)S(1)}, f32[4,4,1,1024]{3,2,1,0:T(1,128)S(1)}, u32[]{:S(2)}, u32[]{:S(2)}) collective-permute-start(f32[4,4,1,1024]{3,2,1,0:T(1,128)S(1)} %get-tuple-element.20), channel_id=1, source_target_pairs={{1,0},{2,1},{3,2},{4,3},{5,4},{6,5},{7,6},{8,7},{9,8},{10,9},{11,1... | collective-permute-start | bytes 196616 | tf_op jit(solution)/shard_map/ppermute | solution.py:15
Sparse Core Ops, SparseCore 0:
  19.2 49.3 all-gather.1
where the time goes:
time: 109 us
  waiting for transfers between devices  42.9 us (39%)
  local copies, waits for them, and re-layouts  15.9 us (15%)
  between operations  13.7 us (13%)
  other arithmetic  13.4 us (12%)
  matrix products  13.4 us (12%)
  starting transfers between devices  9.98 us (9%)
    all_gather x1, waiting for transfers between devices, shards(): lax.all_gather(modes_ext, 'mode', axis=0, tiled=True)[:, None]  37.6 us
    dot_general x1, matrix products, shards(): jnp.einsum('ajk,jkpxy->apxy', my_rows, terms, precision=lax.Precision.HIG...  12.6 us
    mul x12, local copies, waits for them, and re-layouts, apply_terms(): 0.5 * (centre_coef + other_coef) * (centre_field - other_field)  11.3 us
    mul x2, other arithmetic, apply_terms(): 0.5 * (centre_coef + other_coef) * (centre_field - other_field)  11.2 us
    ppermute x2, starting transfers between devices, padded(): before = lax.ppermute(last, axis, up)  7.36 us
    ppermute x2, waiting for transfers between devices, padded(): after = lax.ppermute(initial, axis, down)  5.32 us
    ppermute x2, starting transfers between devices, padded(): after = lax.ppermute(initial, axis, down)  2.58 us
  transfers between devices with their start and end apart: 5, of which 3 were waited for; matrix products, arithmetic and copies ran while one was open for 6% of the time, Pallas kernels for 0%

commit v1 on v0

v1 whole, which is shorter than its diff:
```python
import functools

import jax
import jax.numpy as jnp
from jax import lax
from jax.experimental import pallas as pl
from jax.experimental.pallas import tpu as pltpu
from jax.sharding import PartitionSpec as P

MESH = pl.DeviceIdType.MESH
EVENS = 7
SLOTS = 20
GROUP = 5
CHIP = 10
TERMS = 4
ENTRIES = 80


def tables(high, core, coupling, values, assignment):
    i32 = jnp.int32
    rows, lanes = ENTRIES, 128
    lane = lax.broadcasted_iota(i32, (rows, lanes), 1)
    sub = lax.broadcasted_iota(i32, (rows, lanes), 0)
    slot = lane[0:1]
    first, second, term = coupling[:, 0:1], coupling[:, 1:2], coupling[:, 2:3]
    value = jnp.sum(jnp.where(lane == sub, values, 0.0), axis=1, keepdims=True)
    real = lane < SLOTS
    hit_first = jnp.logical_and(first == assignment, real)
    hit_second = jnp.logical_and(second == assignment, real)
    joined = jnp.logical_and(hit_first, term > 0)
    degree = jnp.sum(jnp.where(joined, 1, 0), axis=0, keepdims=True)
    five = jnp.where(degree == 5, 1, 0)
    by_five = jnp.sum(jnp.where(hit_second, five, 0), axis=1, keepdims=True)
    near_five = jnp.sum(jnp.where(joined, by_five, 0), axis=0, keepdims=True)
    odd = jnp.logical_or(degree <= 2, near_five > 0)
    even = jnp.where(odd, 0, jnp.where(slot < SLOTS, 1, 0))
    lane24, sub24 = lane[:24], sub[:24]
    even_col = jnp.sum(jnp.where(lane24 == sub24, even, 0), axis=1, keepdims=True)
    ahead = jnp.sum(jnp.where(sub24 < lane24, even_col, 0), axis=0, keepdims=True)
    low = jnp.sum(jnp.where(sub24 < CHIP, even_col, 0), axis=0, keepdims=True)
    order0 = ahead
    order1 = jnp.where(slot < CHIP, ahead + (EVENS - low), ahead - low)
    mine = jnp.where(high == 0, order0, order1)
    theirs = jnp.where(high == 0, order1, order0)
    key_row = jnp.where(even > 0, mine, 99)
    key_col = jnp.sum(jnp.where(lane24 == sub24, key_row, 0), axis=1, keepdims=True)
    slot_of = jnp.sum(jnp.where(key_col == lane24, jnp.where(sub24 < SLOTS, sub24, 0), 0), axis=0, keepdims=True)
    local = slot - high * CHIP
    here = jnp.logical_and(local >= 0, local < CHIP)
    place = jnp.where(core == 0, local, jnp.where(local < GROUP, local + GROUP, local - GROUP))
    place = jnp.where(here, place, 0)
    code = slot * 4096 + theirs * 256 + place * 16 + even * 2 + jnp.where(here, 1, 0)
    code_of = jnp.sum(jnp.where(hit_second, code, 0), axis=1, keepdims=True)
    l_index, l_weight, r_index, r_weight = [], [], [], []
    for k in range(1, TERMS):
        chosen = jnp.logical_and(hit_first, term == k)
        lower = jnp.min(jnp.where(chosen, code_of, 1 << 24), axis=0, keepdims=True)
        upper = jnp.max(jnp.where(chosen, code_of, -1), axis=0, keepdims=True)
        upper = jnp.where(upper == lower, -1, upper)
        for found, there in ((lower, lower < (1 << 24)), (upper, upper >= 0)):
            weight = jnp.sum(jnp.where(jnp.logical_and(chosen, code_of == found), value, 0.0), axis=0, keepdims=True)
            is_here = (found % 2) == 1
            is_even = ((found // 2) % 2) == 1
            use_l = jnp.logical_and(there, is_here)
            use_r = jnp.logical_and(there, jnp.logical_and(is_even, jnp.logical_not(is_here)))
            l_index.append(jnp.where(use_l, (found // 16) % 16, 0))
            l_weight.append(jnp.where(use_l, weight, 0.0))
            r_index.append(jnp.where(use_r, (found // 256) % 16, 0))
            r_weight.append(jnp.where(use_r, weight, 0.0))
    diagonal = jnp.sum(jnp.where(jnp.logical_and(hit_first, term == 0), value, 0.0), axis=0, keepdims=True)
    zero_i = jnp.zeros_like(slot)
    zero_f = jnp.zeros_like(diagonal)
    theirs = jnp.where(even > 0, theirs, 0)
    ints = jnp.concatenate(l_index + r_index + [theirs, slot_of, place, zero_i], axis=0)
    floats = jnp.concatenate(l_weight + r_weight + [jnp.where(even > 0, 1.0, 0.0), diagonal, zero_f, zero_f], axis=0)
    return ints, floats


def kernel(
    spaces, sure,
    modes, coefs, coupling, values, assignment, out,
    m, c, es, er, gy, gx, gz, db, gh, ak, dh, sb, rb, hs, hr, dr, akr, acc, tiv, tfv, ti, tf,
    load_sem, table_sem, sib_s, sib_r, edge_s, edge_r, item_s, item_r, plane_s, plane_r, fwd_s, fwd_r, res_sem, res_s, res_r,
):
    f32 = jnp.float32
    mode, space = lax.axis_index("mode"), lax.axis_index("space")
    high, core = mode // 2, mode % 2
    sibling = (high * 2 + (1 - core), space)
    partner = ((1 - high) * 2 + core, space)
    has_low, has_high = space > 0, space < spaces - 1
    width = modes.shape[3]
    maybe = EVENS - sure
    groups = [list(range(maybe))[i : i + 4] for i in range(0, maybe, 4)]
    planes = (3 * core, 1 + core, 2 - core, 3 - 3 * core)

    loads = []
    for at, plane in enumerate(planes):
        loads.append(pltpu.make_async_copy(modes.at[:, pl.ds(plane, 1)], m.at[pl.ds(0, GROUP), pl.ds(at, 1)], load_sem.at[0, at]))
        loads.append(pltpu.make_async_copy(coefs.at[:, pl.ds(plane, 1)], c.at[:, pl.ds(at, 1)], load_sem.at[1, at]))
    for copy in loads:
        copy.start()

    barrier = pltpu.get_barrier_semaphore()
    for target in (sibling, partner):
        pl.semaphore_signal(barrier, inc=1, device_id=target, device_id_type=MESH)
    for there, step in ((has_low, -1), (has_high, 1)):
        @pl.when(there)
        def _():
            for who in (mode, sibling[0]):
                pl.semaphore_signal(barrier, inc=1, device_id=(who, space + step), device_id_type=MESH)

    ints, floats = tables(high, core, coupling[...], values[...], assignment[...])
    tiv[...] = ints
    tfv[...] = floats
    table_copies = [
        pltpu.make_async_copy(tiv, ti, table_sem.at[0]),
        pltpu.make_async_copy(tfv, tf, table_sem.at[1]),
    ]
    for copy in table_copies:
        copy.start()

    for copy in loads:
        copy.wait()

    for side, row in ((0, 7), (1, 0)):
        for other, held in ((0, (0, 1)), (1, (3, 2))):
            for p in range(2):
                for i in range(GROUP):
                    es[side, other, pl.ds(i * 2 + p, 1), :] = m[i, held[p], pl.ds(row, 1), :]
                for kk in range(2):
                    es[side, other, pl.ds(10 + kk * 2 + p, 1), :] = c[2 * core + kk, held[p], pl.ds(row, 1), :]

    for there, side in ((has_low, 0), (has_high, 1)):
        @pl.when(jnp.logical_not(there))
        def _():
            er[side] = jnp.zeros(er.shape[1:], f32)
            hr[side] = jnp.zeros(hr.shape[1:], f32)

    pl.semaphore_wait(barrier, 2 + 2 * has_low.astype(jnp.int32) + 2 * has_high.astype(jnp.int32))

    theirs = (3 - 3 * core, 2 - core, 1 + core)
    to_sibling = [
        pltpu.make_async_remote_copy(
            modes.at[:, pl.ds(plane, 1)], m.at[pl.ds(GROUP, GROUP), pl.ds(at, 1)],
            sib_s.at[at], sib_r.at[at], device_id=sibling, device_id_type=MESH,
        )
        for at, plane in enumerate(theirs)
    ]
    for copy in to_sibling:
        copy.start()

    def edge_copy(side, other, source):
        who = mode if other == 0 else sibling[0]
        return pltpu.make_async_remote_copy(
            es.at[side, other], er.at[side, source], edge_s.at[side, other], edge_r.at[side, source],
            device_id=(who, space + (1 if side == 0 else -1)), device_id_type=MESH,
        )

    for there, side in ((has_high, 0), (has_low, 1)):
        @pl.when(there)
        def _():
            for other in range(2):
                edge_copy(side, other, core).start()

    row = lax.broadcasted_iota(jnp.int32, (8, width), 0)
    col = lax.broadcasted_iota(jnp.int32, (8, width), 1)
    for k in range(TERMS):
        a0, a1, ah = 0.5 * c[k, 0], 0.5 * c[k, 1], 0.5 * c[k, 2]
        for p, a in ((0, a0), (1, a1)):
            gy[k, p] = jnp.where(col == 0, 0.0, a + pltpu.roll(a, 1, 1))
            gx[k, p] = jnp.where(row == 0, 0.0, a + pltpu.roll(a, 1, 0))
        side = jnp.where(jnp.logical_or(col == 0, col == width - 1), 1.0, 0.0)
        db[k, 0] = a0 * (1.0 + side)
        db[k, 1] = a1 * side
        gz[k, 0] = a0 + a1
        gz[k, 1] = a1 + ah

    def stencil(v0, v1, vh, terms, store):
        d0, d1 = v0 - v1, v1 - vh
        y0, y1 = v0 - pltpu.roll(v0, 1, 1), v1 - pltpu.roll(v1, 1, 1)
        x0, x1 = v0 - pltpu.roll(v0, 1, 0), v1 - pltpu.roll(v1, 1, 0)
        for k in terms:
            between = gz[k, 0] * d0
            f = gy[k, 0] * y0
            g = gx[k, 0] * x0
            store(k, 0, (f - pltpu.roll(f, width - 1, 1)) + (g - pltpu.roll(g, 7, 0)) + (between + db[k, 0] * v0))
            f = gy[k, 1] * y1
            g = gx[k, 1] * x1
            store(k, 1, (f - pltpu.roll(f, width - 1, 1)) + (g - pltpu.roll(g, 7, 0)) + (gz[k, 1] * d1 + db[k, 1] * v1 - between))

    def own_stencil(b, carry):
        def store(k, p, value):
            ak[b * TERMS + k, p] = value
        stencil(m[b, 0], m[b, 1], m[b, 2], range(TERMS), store)
        return carry

    lax.fori_loop(0, GROUP, own_stencil, 0)
    for copy in table_copies:
        copy.wait()
    for copy in to_sibling:
        copy.wait_recv()

    def item_copy(j):
        return pltpu.make_async_remote_copy(
            sb.at[j], rb.at[j, pl.ds(0, 2)], item_s.at[j], item_r.at[j], device_id=partner, device_id_type=MESH
        )

    def raw_place(j):
        slot = ti[13, j]
        return slot, ti[14, slot], jnp.where(slot // CHIP == high, 1.0, 0.0).astype(f32)

    for j in range(sure):
        slot, place, ours = raw_place(j)
        for p in range(2):
            sb[j, p] = m[place, p]
        item_copy(j).start()

    lax.fori_loop(GROUP, CHIP, own_stencil, 0)

    for there, side in ((has_low, 0), (has_high, 1)):
        @pl.when(there)
        def _():
            for source in range(2):
                edge_copy(side, 0, source).wait_recv()

    def tile(top0, top1, bottom0, bottom1):
        return jnp.where(row == 0, top0, jnp.where(row == 7, bottom0, jnp.where(row == 4, top1, bottom1)))

    def own_edges(v0, v1):
        return jnp.where(jnp.logical_or(row == 0, row == 7), v0, pltpu.roll(v1, 4, 0))

    def arrived(ref, lead, r):
        return [ref[(side,) + lead + (pl.ds(r + p, 1), slice(None))] for side in range(2) for p in range(2)]

    for k in range(TERMS):
        gh[k] = 0.5 * (own_edges(c[k, 0], c[k, 1]) + tile(*arrived(er, (k // 2,), 10 + (k % 2) * 2)))
    for b in range(CHIP):
        source = core if b < GROUP else 1 - core
        dh[b] = own_edges(m[b, 0], m[b, 1]) - tile(*arrived(er, (source,), (b % GROUP) * 2))

    outer = jnp.logical_or(row == 0, row == 7)

    def spread(packed):
        return jnp.where(outer, packed, 0.0), jnp.where(outer, pltpu.roll(packed, 4, 0), 0.0)

    def gathered(slot, first, applied, stride, shift, edges, scale, starts):
        total0, total1, packed = starts
        for k in range(1, TERMS):
            along = None
            for side in range(2):
                at = first + (k - 1) * 2 + side
                index = ti[at, slot]
                weight = tf[at, slot] * scale
                total0 = total0 + weight * applied[index * stride + (k - shift), 0]
                total1 = total1 + weight * applied[index * stride + (k - shift), 1]
                part = weight * edges[index]
                along = part if along is None else along + part
            packed = gh[k] * along if packed is None else packed + gh[k] * along
        edge0, edge1 = spread(packed)
        return total0 + edge0, total1 + edge1

    for j in range(sure, EVENS):
        slot, place, ours = raw_place(j)
        starts = (ours * m[place, 0], ours * m[place, 1], None)
        sb[j, 0], sb[j, 1] = gathered(slot, 0, ak, TERMS, 0, dh, 1.0 - ours, starts)
        item_copy(j).start()

    def slot_at(b):
        return high * CHIP + jnp.where(b < GROUP, core * GROUP + b, (1 - core) * GROUP + b - GROUP)

    def local_sum(b, carry):
        slot = slot_at(b)
        weight = tf[13, slot]
        starts = (weight * ak[b * TERMS, 0], weight * ak[b * TERMS, 1], gh[0] * (weight * dh[b]))
        acc[b, 0], acc[b, 1] = gathered(slot, 0, ak, TERMS, 0, dh, 1.0, starts)
        return carry

    lax.fori_loop(0, CHIP, local_sum, 0)

    def plane_copy(j):
        return pltpu.make_async_remote_copy(
            rb.at[j, pl.ds(1, 1)], rb.at[j, pl.ds(2, 1)], plane_s.at[j], plane_r.at[j], device_id=sibling, device_id_type=MESH
        )

    def edge_on(side, g):
        return pltpu.make_async_remote_copy(
            hs.at[side, g], hr.at[side, g], fwd_s.at[side, g], fwd_r.at[side, g],
            device_id=(mode, space + (1 if side == 0 else -1)), device_id_type=MESH,
        )

    for g, members in enumerate(groups):
        for n, j in enumerate(members):
            item_copy(j).wait_recv()
            plane_copy(j).start()
            for side, r in ((0, 7), (1, 0)):
                for p in range(2):
                    hs[side, g, pl.ds(n * 2 + p, 1), :] = rb[j, p, pl.ds(r, 1), :]
        for there, side in ((has_high, 0), (has_low, 1)):
            @pl.when(there)
            def _():
                edge_on(side, g).start()

    def raw_stencil(j, carry):
        def store(k, p, value):
            akr[j * 3 + k - 1, p] = value
        stencil(rb[j, 0], rb[j, 1], rb[j, 2], range(1, TERMS), store)
        return carry

    for g, members in enumerate(groups):
        for j in members:
            plane_copy(j).wait_recv()
        lax.fori_loop(members[0], members[-1] + 1, raw_stencil, 0)
        for there, side in ((has_low, 0), (has_high, 1)):
            @pl.when(there)
            def _():
                edge_on(side, g).wait_recv()
        for n, j in enumerate(members):
            dr[j] = own_edges(rb[j, 0], rb[j, 1]) - tile(*arrived(hr, (g,), n * 2))

    def remote_sum(b, carry):
        slot = slot_at(b)
        index = ti[12, slot]
        early = index < maybe
        weight = jnp.where(early, tf[12, slot], 0.0)
        index = jnp.where(early, index, 0)
        starts = (acc[b, 0] + weight * rb[index, 0], acc[b, 1] + weight * rb[index, 1], None)
        acc[b, 0], acc[b, 1] = gathered(slot, 6, akr, 3, 1, dr, 1.0, starts)
        return carry

    lax.fori_loop(0, CHIP, remote_sum, 0)

    results = [
        pltpu.make_async_remote_copy(
            acc.at[pl.ds(GROUP, GROUP), pl.ds(p, 1)], out.at[:, pl.ds(planes[p], 1)], res_s.at[p], res_r.at[p],
            device_id=sibling, device_id_type=MESH,
        )
        for p in range(2)
    ] + [
        pltpu.make_async_copy(acc.at[pl.ds(0, GROUP), pl.ds(p, 1)], out.at[:, pl.ds(planes[p], 1)], res_sem.at[p])
        for p in range(2)
    ]
    for copy in results:
        copy.start()

    for copy in to_sibling:
        copy.wait_send()
    for there, side in ((has_high, 0), (has_low, 1)):
        @pl.when(there)
        def _():
            for other in range(2):
                edge_copy(side, other, core).wait_send()
            for g in range(len(groups)):
                edge_on(side, g).wait_send()
    for j in range(EVENS):
        item_copy(j).wait_send()
    for j in range(maybe):
        plane_copy(j).wait_send()
    for p in range(2):
        results[p].wait_send()
        results[2 + p].wait()
        pltpu.make_async_remote_copy(
            acc.at[pl.ds(GROUP, GROUP), pl.ds(p, 1)], out.at[:, pl.ds(theirs[p], 1)], res_s.at[p], res_r.at[p],
            device_id=sibling, device_id_type=MESH,
        ).wait_recv()


def galerkin(spaces, sure, collective, modes, coefs, coupling, values, assignment):
    width = modes.shape[3]
    f32 = jnp.float32
    maybe = EVENS - sure
    groups = -(-maybe // 4)
    dma = pltpu.SemaphoreType.DMA
    vmem = pltpu.VMEM
    scratch = [
        vmem((CHIP, 4, 8, width), f32),
        vmem((TERMS, 4, 8, width), f32),
        vmem((2, 2, 16, width), f32),
        vmem((2, 2, 16, width), f32),
        vmem((TERMS, 2, 8, width), f32),
        vmem((TERMS, 2, 8, width), f32),
        vmem((TERMS, 2, 8, width), f32),
        vmem((TERMS, 2, 8, width), f32),
        vmem((TERMS, 8, width), f32),
        vmem((CHIP * TERMS, 2, 8, width), f32),
        vmem((CHIP, 8, width), f32),
        vmem((EVENS, 2, 8, width), f32),
        vmem((EVENS, 3, 8, width), f32),
        vmem((2, groups, 8, width), f32),
        vmem((2, groups, 8, width), f32),
        vmem((maybe, 8, width), f32),
        vmem((maybe * 3, 2, 8, width), f32),
        vmem((CHIP, 2, 8, width), f32),
        vmem((16, 128), jnp.int32),
        vmem((16, 128), f32),
        pltpu.SMEM((16, 128), jnp.int32),
        pltpu.SMEM((16, 128), f32),
        dma((2, 4)), dma((2,)), dma((3,)), dma((3,)), dma((2, 2)), dma((2, 2)), dma((EVENS,)), dma((EVENS,)),
        dma((maybe,)), dma((maybe,)), dma((2, groups)), dma((2, groups)), dma((2,)), dma((2,)), dma((2,)),
    ]
    anywhere = pl.BlockSpec(memory_space=pl.ANY)
    held = pl.BlockSpec(memory_space=pltpu.VMEM)
    return pl.pallas_call(
        functools.partial(kernel, spaces, sure),
        out_shape=jax.ShapeDtypeStruct(modes.shape, f32),
        in_specs=[anywhere, anywhere, held, held, held],
        out_specs=anywhere,
        scratch_shapes=scratch,
        compiler_params=pltpu.CompilerParams(
            collective_id=collective, has_side_effects=True, vmem_limit_bytes=32 * 1024 * 1024
        ),
        name="galerkin",
    )(modes, coefs, coupling, values, assignment)


def solution(mesh):
    spaces = mesh.shape["space"]

    def shards(modes, coefficients, coupling, coupling_values, assignment):
        pad = 128 - assignment.shape[0]
        values = jnp.pad(coupling_values, (0, 128 - coupling_values.shape[0]))[None]
        held = jnp.pad(assignment, (0, pad), constant_values=-1)[None]
        return galerkin(spaces, 0, 0, modes, coefficients, coupling, values, held)

    in_specs = (P("mode", None, "space", None), P(None, None, "space", None), P(), P(), P())
    out_specs = P("mode", None, "space", None)
    return jax.shard_map(shards, mesh=mesh, in_specs=in_specs, out_specs=out_specs, check_vma=False)
```

time: 109 us -> 45.7 us (0.42)
  the two profiles are of different devices: /device:TPU:1 before, /device:TPU:9 now
where the time goes in v1:
time: 45.7 us; the launch traced here: 45.5 us
  Pallas kernels  41.7 us (91%)
  local copies, waits for them, and re-layouts  3.76 us (8%)
    pallas_call x1, Pallas kernels, galerkin(): pl.pallas_call(functools.partial(kernel, spaces, sure), out_shape=jax.Sha...  41.7 us
    unnamed x10, local copies, waits for them, and re-layouts  3.07 us

profile of v1, /device:TPU:9, one launch (start us, length us, event | category | flops | bytes accessed | tf_op | source)
XLA Modules:
  0.0 45.5 jit_solution(15221749467954928708)
XLA Ops:
  0.0 0.0 copy-start.3
  0.0 0.0 copy-start.2
  0.0 0.7 %pad_bitcast_fusion.1.values = f32[1,128]{1,0:T(1,128)S(1)} fusion(f32[80]{0:T(128)} %param.8), kind=kLoop, calls=%fused_computation.1 | loop fusion | bytes 832 | tf_op jit(solution)/shard_map/broadcast_in_dim | solution.py:420
  0.7 0.0 copy-done.3
  0.7 0.0 copy-done.2
  0.7 0.1 copy.6.coupling
  0.8 0.0 copy-start
  0.8 1.1 %copy-done = f32[5,4,8,1024]{3,2,1,0:T(8,128)S(1)} copy-done((f32[5,4,8,1024]{3,2,1,0:T(8,128)S(1)}, f32[5,4,8,1024]{3,2,1,0:T(8,128)}, u32[]{:S(2)}) %copy-start) | copy-done | bytes 655384
  1.9 0.0 copy-start.1
  1.9 1.0 %copy-done.1 = f32[4,4,8,1024]{3,2,1,0:T(8,128)S(1)} copy-done((f32[4,4,8,1024]{3,2,1,0:T(8,128)S(1)}, f32[4,4,8,1024]{3,2,1,0:T(8,128)}, u32[]{:S(2)}) %copy-start.1) | copy-done | bytes 524312
  2.9 41.7 %galerkin.1 = f32[5,4,8,1024]{3,2,1,0:T(8,128)S(1)} custom-call(f32[5,4,8,1024]{3,2,1,0:T(8,128)S(1)} %copy-done, f32[4,4,8,1024]{3,2,1,0:T(8,128)S(1)} %copy-done.1, s32[80,3]{1,0:T(8,128)S(1)} %copy.6.coupling, f32[1,128]{1,0:T(1,128)S(1)} %pad_bitcast_fusion.1.values, s32[1,128]{1,0:T(1,128)S(1)} %pad_bitcast_fusion.assignment), custom_call_target="tpu_custom_call" | custom-call | tf_op jit(solution)/shard_map/galerkin/pallas_call | solution.py:402
  44.7 0.8 %copy.8 = f32[5,4,8,1024]{3,2,1,0:T(8,128)} copy(f32[5,4,8,1024]{3,2,1,0:T(8,128)S(1)} %galerkin.1) | data formatting | bytes 1310720
  (1 shorter events, 0.0 us)
Async XLA Ops:
  0.0 0.7 %copy-start.3 = (s32[20]{0:T(128)S(1)}, s32[20]{0:T(128)}, u32[]{:S(2)}) copy-start(s32[20]{0:T(128)} %param.9) | copy-start | bytes 244
  0.0 0.7 %copy-start.2 = (s32[80,3]{0,1:T(4,128)S(1)}, s32[80,3]{0,1:T(4,128)}, u32[]{:S(2)}) copy-start(s32[80,3]{0,1:T(4,128)} %param.7) | copy-start | bytes 2884
  0.8 1.1 %copy-start = (f32[5,4,8,1024]{3,2,1,0:T(8,128)S(1)}, f32[5,4,8,1024]{3,2,1,0:T(8,128)}, u32[]{:S(2)}) copy-start(f32[5,4,8,1024]{3,2,1,0:T(8,128)} %modes.1) | copy-start | bytes 1966084
  1.9 1.0 %copy-start.1 = (f32[4,4,8,1024]{3,2,1,0:T(8,128)S(1)}, f32[4,4,8,1024]{3,2,1,0:T(8,128)}, u32[]{:S(2)}) copy-start(f32[4,4,8,1024]{3,2,1,0:T(8,128)} %coefs.1) | copy-start | bytes 1572868

commit v2 on v1

v2 whole, which is shorter than its diff:
```python
import functools

import jax
import jax.numpy as jnp
from jax import lax
from jax.experimental import pallas as pl
from jax.experimental.pallas import tpu as pltpu
from jax.sharding import PartitionSpec as P

MESH = pl.DeviceIdType.MESH
EVENS = 7
SLOTS = 20
GROUP = 5
CHIP = 10
TERMS = 4
ENTRIES = 80
EARLY = 2
LATE = EVENS - 2
ENDS = EVENS - LATE
INF = 1 << 24


def tables(high, core, coupling, values, assignment):
    i32 = jnp.int32
    slot = lax.broadcasted_iota(i32, (1, SLOTS), 1)
    lane = lax.broadcasted_iota(i32, (SLOTS, SLOTS), 1)
    sub = lax.broadcasted_iota(i32, (SLOTS, SLOTS), 0)
    eye = lax.broadcasted_iota(i32, (ENTRIES, ENTRIES), 0) == lax.broadcasted_iota(i32, (ENTRIES, ENTRIES), 1)
    first, second, term = [jnp.sum(jnp.where(eye, coupling[n : n + 1], 0), axis=1, keepdims=True) for n in range(3)]
    value = jnp.sum(jnp.where(eye, values, 0.0), axis=1, keepdims=True)
    hit_first = first == assignment
    hit_second = second == assignment
    joined = jnp.logical_and(hit_first, term > 0)
    degree = jnp.sum(jnp.where(joined, 1, 0), axis=0, keepdims=True)
    five = jnp.where(degree == 5, 1, 0)
    by_five = jnp.sum(jnp.where(hit_second, five, 0), axis=1, keepdims=True)
    near_five = jnp.sum(jnp.where(joined, by_five, 0), axis=0, keepdims=True)
    even = jnp.where(jnp.logical_or(degree <= 2, near_five > 0), 0, 1)
    even_col = jnp.sum(jnp.where(lane == sub, even, 0), axis=1, keepdims=True)
    ahead = jnp.sum(jnp.where(sub < lane, even_col, 0), axis=0, keepdims=True)
    low = jnp.sum(jnp.where(sub < CHIP, even_col, 0), axis=0, keepdims=True)
    order0 = ahead
    order1 = jnp.where(slot < CHIP, ahead + (EVENS - low), ahead - low)
    mine = jnp.where(high == 0, order0, order1)
    theirs = jnp.where(high == 0, order1, order0)
    key_row = jnp.where(even > 0, mine, 99)
    key_col = jnp.sum(jnp.where(lane == sub, key_row, 0), axis=1, keepdims=True)
    slot_of = jnp.sum(jnp.where(key_col == lane, sub, 0), axis=0, keepdims=True)
    local = slot - high * CHIP
    here = jnp.logical_and(local >= 0, local < CHIP)
    place = jnp.where(core == 0, local, jnp.where(local < GROUP, local + GROUP, local - GROUP))
    place = jnp.where(here, place, CHIP + slot - (1 - high) * CHIP)
    code = slot * 8192 + theirs * 512 + place * 16 + even * 2 + jnp.where(here, 1, 0)
    code_of = jnp.sum(jnp.where(hit_second, code, 0), axis=1, keepdims=True)
    l_index, l_weight, r_index, r_weight, a_index, a_weight = [], [], [], [], [], []
    for k in range(1, TERMS):
        chosen = jnp.logical_and(hit_first, term == k)
        lower = jnp.min(jnp.where(chosen, code_of, INF), axis=0, keepdims=True)
        upper = jnp.max(jnp.where(chosen, code_of, -1), axis=0, keepdims=True)
        upper = jnp.where(upper == lower, -1, upper)
        for found, there in ((lower, lower < INF), (upper, upper >= 0)):
            weight = jnp.sum(jnp.where(jnp.logical_and(chosen, code_of == found), value, 0.0), axis=0, keepdims=True)
            is_here = (found % 2) == 1
            is_even = ((found // 2) % 2) == 1
            use_l = jnp.logical_and(there, is_here)
            use_r = jnp.logical_and(there, jnp.logical_and(is_even, jnp.logical_not(is_here)))
            l_index.append(jnp.where(use_l, (found // 16) % 32, 0))
            l_weight.append(jnp.where(use_l, weight, 0.0))
            r_index.append(jnp.where(use_r, (found // 512) % 16, 0))
            r_weight.append(jnp.where(use_r, weight, 0.0))
            a_index.append(jnp.where(there, (found // 16) % 32, 0))
            a_weight.append(jnp.where(there, weight, 0.0))
    diagonal = jnp.sum(jnp.where(jnp.logical_and(hit_first, term == 0), value, 0.0), axis=0, keepdims=True)
    zero_i = jnp.zeros_like(slot)
    zero_f = jnp.zeros_like(diagonal)
    theirs = jnp.where(even > 0, theirs, 0)
    place = jnp.where(here, place, 0)

    def within(rows, size):
        return [jnp.clip(x, 0, size - 1) for x in rows]

    l_index, r_index, a_index = within(l_index, CHIP), within(r_index, EVENS), within(a_index, SLOTS)
    ints = within([theirs], EVENS) + within([slot_of], SLOTS) + within([place], CHIP) + [zero_i]
    floats = [jnp.where(even > 0, 1.0, 0.0), diagonal, zero_f, zero_f]
    ints = jnp.concatenate(l_index + r_index + ints + a_index + [zero_i, zero_i], axis=0)
    floats = jnp.concatenate(l_weight + r_weight + floats + a_weight + [zero_f, zero_f], axis=0)
    return ints, floats


def kernel(
    spaces,
    modes, coefs, coupling, values, assignment, out,
    m, c, es, er, gy, gx, gz, db, gh, ak, dh, sb, rb, ts, tr, hs, hr, dr, akr, acc, sh, se, ds, gs,
    rl, akl, drl, ghf, trf, drf, far,
    cv, vv, av, tiv, tfv, ti, tf,
    load_sem, small_sem, table_sem, sib_s, sib_r, edge_s, edge_r, item_s, item_r, tile_s, tile_r, plane_s, plane_r,
    fwd_s, fwd_r, seam_s, seam_r, pair_s, pair_r, outer_s, outer_r, give_s, give_r,
):
    f32, i32 = jnp.float32, jnp.int32
    mode, space = lax.axis_index("mode"), lax.axis_index("space")
    high, core = mode // 2, mode % 2
    half = spaces // 2
    low_seam, high_seam = space < 0, space < 0
    seam = jnp.logical_or(low_seam, high_seam)
    has_low = jnp.logical_and(space > 0, jnp.logical_not(low_seam))
    has_high = jnp.logical_and(space < spaces - 1, jnp.logical_not(high_seam))
    across = jnp.where(low_seam, space - 1, space + 1)
    sibling_mode = high * 2 + (1 - core)
    sibling = (sibling_mode, space)
    partner = ((1 - high) * 2 + core, space)
    diagonal = ((1 - high) * 2 + (1 - core), space)
    width = modes.shape[3]
    groups = [list(range(LATE))[i : i + 4] for i in range(0, LATE, 4)]
    planes = (3 * core, 1 + core, 2 - core, 3 - 3 * core)
    theirs = (3 - 3 * core, 2 - core, 1 + core)
    ups = ((has_high, 0), (has_low, 1))
    downs = ((has_low, 0), (has_high, 1))

    def signal(target):
        pl.semaphore_signal(barrier, inc=1, device_id=target, device_id_type=MESH)

    barrier = pltpu.get_barrier_semaphore()
    signal(sibling)
    signal(partner)
    for there, step in ((has_low, -1), (has_high, 1)):
        @pl.when(there)
        def _():
            for who in (mode, sibling_mode):
                signal((who, space + step))

    @pl.when(seam)
    def _():
        signal(diagonal)

    @pl.when(low_seam)
    def _():
        for who in range(4):
            signal((who, space - 1))

    loads = []
    for at, plane in enumerate(planes):
        loads.append(pltpu.make_async_copy(modes.at[:, pl.ds(plane, 1)], m.at[pl.ds(0, GROUP), pl.ds(at, 1)], load_sem.at[0, at]))
        loads.append(pltpu.make_async_copy(coefs.at[:, pl.ds(plane, 1)], c.at[:, pl.ds(at, 1)], load_sem.at[1, at]))
    smalls = [
        pltpu.make_async_copy(source, target, small_sem.at[n])
        for n, (source, target) in enumerate(((coupling, cv), (values, vv), (assignment, av)))
    ]
    for copy in smalls + loads:
        copy.start()

    peers = 2 + 2 * has_low.astype(i32) + 2 * has_high.astype(i32) + seam.astype(i32) + 4 * high_seam.astype(i32)
    pl.semaphore_wait(barrier, peers)

    to_sibling = [
        pltpu.make_async_remote_copy(
            modes.at[:, pl.ds(plane, 1)], m.at[pl.ds(GROUP, GROUP), pl.ds(at, 1)],
            sib_s.at[at], sib_r.at[at], device_id=sibling, device_id_type=MESH,
        )
        for at, plane in enumerate(theirs)
    ]
    for copy in to_sibling:
        copy.start()

    for copy in smalls:
        copy.wait()
    tiv[...] = jnp.zeros(tiv.shape, i32)
    tfv[...] = jnp.zeros(tfv.shape, f32)
    tiv[:, 0:SLOTS], tfv[:, 0:SLOTS] = tables(high, core, cv[...], vv[...], av[...])
    table_copies = [
        pltpu.make_async_copy(tiv, ti, table_sem.at[0]),
        pltpu.make_async_copy(tfv, tf, table_sem.at[1]),
    ]
    for copy in table_copies:
        copy.start()

    for copy in loads:
        copy.wait()

    for side, row in ((0, 7), (1, 0)):
        for other, held in ((0, (0, 1)), (1, (3, 2))):
            for p in range(2):
                for i in range(GROUP):
                    es[side, other, pl.ds(i * 2 + p, 1), :] = m[i, held[p], pl.ds(row, 1), :]
                for kk in range(2):
                    es[side, other, pl.ds(10 + kk * 2 + p, 1), :] = c[2 * core + kk, held[p], pl.ds(row, 1), :]

    def edge_copy(side, other, source):
        who = mode if other == 0 else sibling_mode
        return pltpu.make_async_remote_copy(
            es.at[side, other], er.at[side, source], edge_s.at[side, other], edge_r.at[side, source],
            device_id=(who, space + (1 if side == 0 else -1)), device_id_type=MESH,
        )

    seam_side = jnp.where(low_seam, 1, 0)

    def seam_copy(chip, other, source):
        who = chip * 2 + (core if other == 0 else 1 - core)
        return pltpu.make_async_remote_copy(
            es.at[seam_side, other], sh.at[source], seam_s.at[chip, other], seam_r.at[source],
            device_id=(who, across), device_id_type=MESH,
        )

    def pair_copy(other, source):
        return pltpu.make_async_remote_copy(
            es.at[seam_side, other], se.at[source], pair_s.at[other], pair_r.at[source],
            device_id=partner if other == 0 else diagonal, device_id_type=MESH,
        )

    @pl.when(high_seam)
    def _():
        for chip in range(2):
            for other in range(2):
                seam_copy(chip, other, mode).start()

    for there, side in ups:
        @pl.when(there)
        def _():
            for other in range(2):
                edge_copy(side, other, core).start()

    @pl.when(seam)
    def _():
        for other in range(2):
            pair_copy(other, core).start()

    for there, side in downs:
        @pl.when(jnp.logical_not(there))
        def _():
            er[side] = jnp.zeros(er.shape[1:], f32)
            hr[side] = jnp.zeros(hr.shape[1:], f32)

    row = lax.broadcasted_iota(i32, (8, width), 0)
    col = lax.broadcasted_iota(i32, (8, width), 1)

    def along_plane(k, p, carry):
        a = 0.5 * c[k, p]
        gy[k, p] = jnp.where(col == 0, 0.0, a + pltpu.roll(a, 1, 1))
        gx[k, p] = jnp.where(row == 0, 0.0, a + pltpu.roll(a, 1, 0))
        side = jnp.where(jnp.logical_or(col == 0, col == width - 1), 1.0, 0.0)
        db[k, p] = a * (side + carry)

    def near_faces(k, carry):
        along_plane(k, 0, 1.0)
        along_plane(k, 1, 0.0)
        gz[k, 0] = 0.5 * (c[k, 0] + c[k, 1])
        gz[k, 1] = 0.5 * (c[k, 1] + c[k, 2])
        return carry

    def far_faces(k, carry):
        along_plane(k, 3, 1.0)
        along_plane(k, 2, 0.0)
        gz[k, 2] = 0.5 * (c[k, 2] + c[k, 3])
        return carry

    def stencil(v, terms, store, far_side=False):
        p0, p1, z0 = (3, 2, 2) if far_side else (0, 1, 0)
        v0, v1, vh = v
        d0, d1 = v0 - v1, v1 - vh
        y0, y1 = v0 - pltpu.roll(v0, 1, 1), v1 - pltpu.roll(v1, 1, 1)
        x0, x1 = v0 - pltpu.roll(v0, 1, 0), v1 - pltpu.roll(v1, 1, 0)
        for k in terms:
            between = gz[k, z0] * d0
            f = gy[k, p0] * y0
            g = gx[k, p0] * x0
            store(k, p0, (f - pltpu.roll(f, width - 1, 1)) + (g - pltpu.roll(g, 7, 0)) + (between + db[k, p0] * v0))
            f = gy[k, p1] * y1
            g = gx[k, p1] * x1
            store(k, p1, (f - pltpu.roll(f, width - 1, 1)) + (g - pltpu.roll(g, 7, 0)) + (gz[k, 1] * d1 + db[k, p1] * v1 - between))

    def own_stencil(b, carry):
        def store(k, p, value):
            ak[b * TERMS + k, p] = value
        stencil((m[b, 0], m[b, 1], m[b, 2]), range(TERMS), store)
        return carry

    lax.fori_loop(0, TERMS, near_faces, 0)
    for copy in table_copies:
        copy.wait()
    for copy in to_sibling:
        copy.wait_recv()

    outer = jnp.logical_or(row == 0, row == 7)
    middle = jnp.logical_or(row == 3, row == 4)
    upper = jnp.logical_or(row == 0, row == 4)

    def spread(packed):
        return jnp.where(outer, packed, 0.0), jnp.where(outer, pltpu.roll(packed, 4, 0), 0.0)

    def inner_sum(slot, scale, totals):
        total0, total1 = totals
        for k in range(1, TERMS):
            for side in range(2):
                at = (k - 1) * 2 + side
                index = ti[at, slot] * TERMS + k
                weight = tf[at, slot] * scale
                total0 = total0 + weight * ak[index, 0]
                total1 = total1 + weight * ak[index, 1]
        return total0, total1

    def edge_sum(slot, first, scale, edges, faces, packed):
        for k in range(1, TERMS):
            at = first + (k - 1) * 2
            along = (tf[at, slot] * scale) * edges[ti[at, slot]] + (tf[at + 1, slot] * scale) * edges[ti[at + 1, slot]]
            packed = faces[k] * along if packed is None else packed + faces[k] * along
        return packed

    def item_copy(j):
        target = rb.at[j, pl.ds(0, 2)] if j < LATE else rl.at[j - LATE, pl.ds(0, 2)]
        return pltpu.make_async_remote_copy(
            sb.at[j], target, item_s.at[j], item_r.at[j], device_id=partner, device_id_type=MESH
        )

    def item_of(j):
        slot = ti[13, j]
        return slot, ti[14, slot], jnp.where(slot // CHIP == high, 1.0, 0.0).astype(f32)

    def slot_at(b):
        return high * CHIP + jnp.where(b < GROUP, core * GROUP + b, (1 - core) * GROUP + b - GROUP)

    def begin_item(j, carry):
        slot, place, ours = item_of(j)
        sb[j, 0], sb[j, 1] = inner_sum(slot, 1.0 - ours, (ours * m[place, 0], ours * m[place, 1]))
        return carry

    def early_item(j):
        slot, place, ours = item_of(j)
        totals = [ours * m[place, 0], ours * m[place, 1]]
        for k in range(1, TERMS):
            at = (k - 1) * 2
            weights = [tf[at + side, slot] * (1.0 - ours) for side in range(2)]
            places = [ti[at + side, slot] for side in range(2)]
            mixed = [weights[0] * m[places[0], p] + weights[1] * m[places[1], p] for p in range(3)]
            def store(_, p, value):
                totals[p] = totals[p] + value
            stencil(mixed, (k,), store)
        sb[j, 0], sb[j, 1] = totals

    for j in range(EARLY):
        early_item(j)
        item_copy(j).start()

    lax.fori_loop(0, CHIP, own_stencil, 0)
    lax.fori_loop(EARLY, EVENS, begin_item, 0)

    for there, side in downs:
        @pl.when(there)
        def _():
            for source in range(2):
                edge_copy(side, 0, source).wait_recv()

    def tile(top0, top1, bottom0, bottom1):
        return jnp.where(row == 0, top0, jnp.where(row == 7, bottom0, jnp.where(row == 4, top1, bottom1)))

    def own_edges(v0, v1):
        return jnp.where(outer, v0, pltpu.roll(v1, 4, 0))

    def arrived(ref, lead, r):
        return [ref[(side,) + lead + (pl.ds(r + p, 1), slice(None))] for side in range(2) for p in range(2)]

    left_out = jnp.logical_or(
        jnp.logical_and(low_seam, upper), jnp.logical_and(high_seam, jnp.logical_or(row == 7, row == 3))
    )
    for k in range(TERMS):
        faces = own_edges(c[k, 0], c[k, 1]) + tile(*arrived(er, (k // 2,), 10 + (k % 2) * 2))
        gh[k] = jnp.where(left_out, 0.0, 0.5 * faces)
    for b in range(CHIP):
        source = core if b < GROUP else 1 - core
        dh[b] = own_edges(m[b, 0], m[b, 1]) - tile(*arrived(er, (source,), (b % GROUP) * 2))

    tile_copy = pltpu.make_async_remote_copy(ts, tr, tile_s, tile_r, device_id=partner, device_id_type=MESH)

    for j in range(EARLY, EVENS):
        slot, place, ours = item_of(j)
        edge0, edge1 = spread(edge_sum(slot, 0, 1.0 - ours, dh, gh, None))
        sb[j, 0] = sb[j, 0] + edge0
        sb[j, 1] = sb[j, 1] + edge1
        item_copy(j).start()
        if j == LATE - 1:
            pair = []
            for n in range(EARLY):
                slot, _, ours = item_of(n)
                _, place, late_ours = item_of(LATE + n)
                pair.append(edge_sum(slot, 0, 1.0 - ours, dh, gh, late_ours * dh[place]))
            moved = jnp.where(jnp.logical_or(row == 1, row == 5), pltpu.roll(pair[1], 1, 0), pltpu.roll(pair[1], 7, 0))
            ts[...] = jnp.where(jnp.logical_or(outer, middle), pair[0], moved)
            tile_copy.start()

    def give(n, source, target):
        return pltpu.make_async_remote_copy(
            source, target, give_s.at[n], give_r.at[n], device_id=sibling, device_id_type=MESH
        )

    faces_copy = give(0, gh, ghf)
    tile_on = give(1, tr, trf)
    sums_copy = give(2, acc.at[pl.ds(GROUP, GROUP)], far)
    faces_copy.start()
    lax.fori_loop(0, TERMS, far_faces, 0)

    def local_sum(b, carry):
        slot = slot_at(b)
        weight = tf[13, slot]
        total0, total1 = inner_sum(slot, 1.0, (weight * ak[b * TERMS, 0], weight * ak[b * TERMS, 1]))
        edge0, edge1 = spread(edge_sum(slot, 0, 1.0, dh, gh, gh[0] * (weight * dh[b])))
        acc[b, 0], acc[b, 1] = total0 + edge0, total1 + edge1
        return carry

    lax.fori_loop(0, CHIP, local_sum, 0)

    def plane_copy(j):
        held, at = (rb, j) if j < LATE else (rl, j - LATE)
        return pltpu.make_async_remote_copy(
            held.at[at, pl.ds(1, 1)], held.at[at, pl.ds(2, 1)], plane_s.at[j], plane_r.at[j],
            device_id=sibling, device_id_type=MESH,
        )

    def outer_copy(n):
        return pltpu.make_async_remote_copy(
            rl.at[n, pl.ds(0, 1)], rl.at[n, pl.ds(3, 1)], outer_s.at[n], outer_r.at[n],
            device_id=sibling, device_id_type=MESH,
        )

    def edge_on(side, g):
        return pltpu.make_async_remote_copy(
            hs.at[side, g], hr.at[side, g], fwd_s.at[side, g], fwd_r.at[side, g],
            device_id=(mode, space + (1 if side == 0 else -1)), device_id_type=MESH,
        )

    def raw_stencil(j, carry):
        def store(k, p, value):
            akr[j * 3 + k - 1, p] = value
        stencil((rb[j, 0], rb[j, 1], rb[j, 2]), range(1, TERMS), store)
        return carry

    for g, members in enumerate(groups):
        for n, j in enumerate(members):
            item_copy(j).wait_recv()
            plane_copy(j).start()
            for side, r in ((0, 7), (1, 0)):
                for p in range(2):
                    hs[side, g, pl.ds(n * 2 + p, 1), :] = rb[j, p, pl.ds(r, 1), :]
        for there, side in ups:
            @pl.when(there)
            def _():
                edge_on(side, g).start()
        for j in members:
            plane_copy(j).wait_recv()
        lax.fori_loop(members[0], members[-1] + 1, raw_stencil, 0)
    def remote_sum(b, carry):
        slot = slot_at(b)
        index = ti[12, slot]
        soon = index < LATE
        weight = jnp.where(soon, tf[12, slot], 0.0)
        at = jnp.minimum(index, LATE - 1)
        total0, total1 = acc[b, 0] + weight * rb[at, 0], acc[b, 1] + weight * rb[at, 1]
        for cell in range(6):
            at = ti[6 + cell, slot]
            weight = jnp.where(at < LATE, tf[6 + cell, slot], 0.0)
            at = jnp.minimum(at, LATE - 1) * 3 + cell // 2
            total0 = total0 + weight * akr[at, 0]
            total1 = total1 + weight * akr[at, 1]
        acc[b, 0], acc[b, 1] = total0, total1
        return carry

    lax.fori_loop(0, CHIP, remote_sum, 0)

    def unpack(ref, target):
        target[0] = ref[...]
        target[1] = jnp.where(upper, pltpu.roll(ref[...], 7, 0), pltpu.roll(ref[...], 1, 0))

    tile_copy.wait_recv()
    tile_on.start()
    unpack(tr, drl)

    for g, members in enumerate(groups):
        for there, side in downs:
            @pl.when(there)
            def _():
                edge_on(side, g).wait_recv()
        for n, j in enumerate(members):
            dr[j] = own_edges(rb[j, 0], rb[j, 1]) - tile(*arrived(hr, (g,), n * 2))

    def remote_edges(b, carry):
        slot = slot_at(b)
        packed = None
        for k in range(1, TERMS):
            along = None
            for side in range(2):
                cell = 6 + (k - 1) * 2 + side
                at = ti[cell, slot]
                part = jnp.where(at < LATE, tf[cell, slot], 0.0) * dr[jnp.minimum(at, LATE - 1)]
                along = part if along is None else along + part
            packed = gh[k] * along if packed is None else packed + gh[k] * along
        edge0, edge1 = spread(packed)
        acc[b, 0] = acc[b, 0] + edge0
        acc[b, 1] = acc[b, 1] + edge1
        return carry

    lax.fori_loop(0, CHIP, remote_edges, 0)

    @pl.when(jnp.logical_not(seam))
    def _():
        sums_copy.start()

    for n in range(ENDS):
        item_copy(LATE + n).wait_recv()
        plane_copy(LATE + n).start()
        outer_copy(n).start()

    @pl.when(seam)
    def _():
        for source in range(4):
            seam_copy(0, 0, source).wait_recv()

        @pl.when(low_seam)
        def _():
            for chip in range(2):
                for other in range(2):
                    seam_copy(chip, other, mode).start()

        for source in range(2):
            pair_copy(0, source).wait_recv()

        def rows(ref, lead, r):
            return jnp.where(outer, ref[lead, pl.ds(r, 1), :], ref[lead, pl.ds(r + 1, 1), :])

        facing = jnp.logical_or(
            jnp.logical_and(low_seam, upper), jnp.logical_and(high_seam, jnp.logical_or(row == 7, row == 3))
        )
        for k in range(TERMS):
            faces = own_edges(c[k, 0], c[k, 1]) + rows(sh, high * 2 + k // 2, 10 + (k % 2) * 2)
            gs[k] = jnp.where(facing, 0.5 * faces, 0.0)
        for b in range(CHIP):
            source = high * 2 + (core if b < GROUP else 1 - core)
            ds[b] = own_edges(m[b, 0], m[b, 1]) - rows(sh, source, (b % GROUP) * 2)
            ds[CHIP + b] = rows(se, b // GROUP, (b % GROUP) * 2) - rows(sh, (1 - high) * 2 + b // GROUP, (b % GROUP) * 2)

        def seam_sum(b, carry):
            slot = slot_at(b)
            edge0, edge1 = spread(edge_sum(slot, 16, 1.0, ds, gs, gs[0] * (tf[13, slot] * ds[b])))
            acc[b, 0] = acc[b, 0] + edge0
            acc[b, 1] = acc[b, 1] + edge1
            return carry

        lax.fori_loop(0, CHIP, seam_sum, 0)
        sums_copy.start()

    def late_stencil(far_side, n):
        def store(k, p, value):
            akl[n * 3 + k - 1, p] = value
        near, mid, beyond = (3, 2, 1) if far_side else (0, 1, 2)
        stencil((rl[n, near], rl[n, mid], rl[n, beyond]), range(1, TERMS), store, far_side)

    for n in range(ENDS):
        plane_copy(LATE + n).wait_recv()
        late_stencil(False, n)
        outer_copy(n).wait_recv()
        late_stencil(True, n)
    faces_copy.wait_recv()
    tile_on.wait_recv()
    unpack(trf, drf)
    sums_copy.wait_recv()

    def late_sum(b, carry):
        slot = slot_at(b)
        index = ti[12, slot]
        late = index >= LATE
        weight = jnp.where(late, tf[12, slot], 0.0)
        at = jnp.maximum(index - LATE, 0)
        totals = [acc[b, 0], acc[b, 1], far[b, 1], far[b, 0]]
        totals = [total + weight * rl[at, p] for p, total in enumerate(totals)]
        near_edge, far_edge = 0.0, 0.0
        for n in range(ENDS):
            weight = jnp.where(index == n, tf[12, slot], 0.0)
            near_edge, far_edge = near_edge + weight * drl[n], far_edge + weight * drf[n]
            weight, term = jnp.float32(0.0), jnp.int32(0)
            for cell in range(6):
                found = ti[6 + cell, slot] == LATE + n
                weight = jnp.where(found, tf[6 + cell, slot], weight)
                term = jnp.where(found, cell // 2, term)
            totals = [total + weight * akl[n * 3 + term, p] for p, total in enumerate(totals)]
            near_edge = near_edge + gh[term + 1] * (weight * drl[n])
            far_edge = far_edge + ghf[term + 1] * (weight * drf[n])
        edges = spread(near_edge) + spread(far_edge)[::-1]
        for p in range(4):
            out[b, planes[p]] = totals[p] + edges[p]
        return carry

    lax.fori_loop(0, GROUP, late_sum, 0)

    for copy in to_sibling:
        copy.wait_send()
    for there, side in ups:
        @pl.when(there)
        def _():
            for other in range(2):
                edge_copy(side, other, core).wait_send()
            for g in range(len(groups)):
                edge_on(side, g).wait_send()

    @pl.when(seam)
    def _():
        for other in range(2):
            pair_copy(other, core).wait_send()
            for chip in range(2):
                seam_copy(chip, other, mode).wait_send()

    for j in range(EVENS):
        item_copy(j).wait_send()
        plane_copy(j).wait_send()
    for n in range(ENDS):
        outer_copy(n).wait_send()
    for copy in (tile_copy, faces_copy, tile_on, sums_copy):
        copy.wait_send()


def galerkin(spaces, modes, coefs, coupling, values, assignment):
    width = modes.shape[3]
    f32 = jnp.float32
    groups = -(-LATE // 4)
    dma = pltpu.SemaphoreType.DMA
    vmem = pltpu.VMEM
    scratch = [
        vmem((CHIP, 4, 8, width), f32),
        vmem((TERMS, 4, 8, width), f32),
        vmem((2, 2, 16, width), f32),
        vmem((2, 2, 16, width), f32),
        vmem((TERMS, 4, 8, width), f32),
        vmem((TERMS, 4, 8, width), f32),
        vmem((TERMS, 4, 8, width), f32),
        vmem((TERMS, 4, 8, width), f32),
        vmem((TERMS, 8, width), f32),
        vmem((CHIP * TERMS, 2, 8, width), f32),
        vmem((CHIP, 8, width), f32),
        vmem((EVENS, 2, 8, width), f32),
        vmem((LATE, 3, 8, width), f32),
        vmem((8, width), f32),
        vmem((8, width), f32),
        vmem((2, groups, 8, width), f32),
        vmem((2, groups, 8, width), f32),
        vmem((LATE, 8, width), f32),
        vmem((LATE * 3, 2, 8, width), f32),
        vmem((CHIP, 2, 8, width), f32),
        vmem((4, 16, width), f32),
        vmem((2, 16, width), f32),
        vmem((SLOTS, 8, width), f32),
        vmem((TERMS, 8, width), f32),
        vmem((ENDS, 4, 8, width), f32),
        vmem((ENDS * 3, 4, 8, width), f32),
        vmem((ENDS, 8, width), f32),
        vmem((TERMS, 8, width), f32),
        vmem((8, width), f32),
        vmem((ENDS, 8, width), f32),
        vmem((GROUP, 2, 8, width), f32),
        vmem(coupling.shape, jnp.int32),
        vmem(values.shape, f32),
        vmem(assignment.shape, jnp.int32),
        vmem((24, 128), jnp.int32),
        vmem((24, 128), f32),
        pltpu.SMEM((24, 128), jnp.int32),
        pltpu.SMEM((24, 128), f32),
        dma((2, 4)), dma((3,)), dma((2,)), dma((3,)), dma((3,)), dma((2, 2)), dma((2, 2)), dma((EVENS,)), dma((EVENS,)),
        dma(()), dma(()), dma((EVENS,)), dma((EVENS,)),
        dma((2, groups)), dma((2, groups)), dma((2, 2)), dma((4,)), dma((2,)), dma((2,)), dma((ENDS,)), dma((ENDS,)),
        dma((3,)), dma((3,)),
    ]
    anywhere = pl.BlockSpec(memory_space=pltpu.HBM)
    return pl.pallas_call(
        functools.partial(kernel, spaces),
        out_shape=jax.ShapeDtypeStruct(modes.shape, f32),
        in_specs=[anywhere] * 5,
        out_specs=pl.BlockSpec(memory_space=pltpu.VMEM),
        scratch_shapes=scratch,
        compiler_params=pltpu.CompilerParams(
            collective_id=0, has_side_effects=True, vmem_limit_bytes=32 * 1024 * 1024
        ),
        name="galerkin",
    )(modes, coefs, coupling, values, assignment)


def solution(mesh):
    spaces = mesh.shape["space"]

    def shards(modes, coefficients, coupling, coupling_values, assignment):
        held = [
            pltpu.with_memory_space_constraint(x, pltpu.HBM)
            for x in (modes, coefficients, coupling.T, coupling_values[None], assignment[None])
        ]
        return galerkin(spaces, *held)

    in_specs = (P("mode", None, "space", None), P(None, None, "space", None), P(), P(), P())
    out_specs = P("mode", None, "space", None)
    return jax.shard_map(shards, mesh=mesh, in_specs=in_specs, out_specs=out_specs, check_vma=False)
```

time: 45.7 us -> 39.2 us (0.86)
  Pallas kernels: 41.7 us -> 38.3 us
  local copies, waits for them, and re-layouts: 3.76 us -> 0.84 us
    pallas_call x1, Pallas kernels: 41.7 us -> 38.3 us  [galerkin(): pl.pallas_call(functools.partial(kernel, spaces), out_shape=jax.ShapeDtyp...]
    unnamed x10 -> x1, local copies, waits for them, and re-layouts: 3.07 us -> 0.84 us
    broadcast_in_dim x2 -> x0, local copies, waits for them, and re-layouts: 0.69 us -> none  [the longest x1 0.68 us: shards(): values = jnp.pad(coupling_values, (0, 128 - coupling_values.shape[0]))[None]]
where the time goes in v2:
time: 39.2 us; the launch traced here: 39.1 us
  Pallas kernels  38.3 us (98%)
  local copies, waits for them, and re-layouts  0.84 us (2%)
    pallas_call x1, Pallas kernels, galerkin(): pl.pallas_call(functools.partial(kernel, spaces), out_shape=jax.ShapeDtyp...  38.3 us
    unnamed x1, local copies, waits for them, and re-layouts  0.84 us

profile of v2, /device:TPU:9, one launch (start us, length us, event | category | flops | bytes accessed | tf_op | source)
XLA Modules:
  0.0 39.1 jit_solution(11342145276816761401)
XLA Ops:
  0.0 38.3 %galerkin.1 = f32[5,4,8,1024]{3,2,1,0:T(8,128)S(1)} custom-call(f32[5,4,8,1024]{3,2,1,0:T(8,128)} %modes.1, f32[4,4,8,1024]{3,2,1,0:T(8,128)} %coefs.1, s32[3,80]{1,0:T(4,128)} %bitcast.3, f32[1,80]{1,0:T(1,128)} %bitcast.4, s32[1,20]{1,0:T(1,128)} %bitcast.5), custom_call_target="tpu_custom_call" | custom-call | tf_op jit(solution)/shard_map/galerkin/pallas_call | solution.py:667
  38.3 0.8 %copy.7 = f32[5,4,8,1024]{3,2,1,0:T(8,128)} copy(f32[5,4,8,1024]{3,2,1,0:T(8,128)S(1)} %galerkin.1) | data formatting | bytes 1310720

commit v3 on v2

--- a/solution.py
+++ b/solution.py
@@ -94,21 +94,22 @@
     rl, akl, drl, ghf, trf, drf, far,
     cv, vv, av, tiv, tfv, ti, tf,
     load_sem, small_sem, table_sem, sib_s, sib_r, edge_s, edge_r, item_s, item_r, tile_s, tile_r, plane_s, plane_r,
-    fwd_s, fwd_r, seam_s, seam_r, pair_s, pair_r, outer_s, outer_r, give_s, give_r,
+    fwd_s, fwd_r, seam_s, seam_r, pair_s, pair_r, outer_s, outer_r, give_s, give_r, ready,
 ):
     f32, i32 = jnp.float32, jnp.int32
     mode, space = lax.axis_index("mode"), lax.axis_index("space")
     high, core = mode // 2, mode % 2
     half = spaces // 2
-    low_seam, high_seam = space < 0, space < 0
+    low_seam, high_seam = space == half, space == half - 1
     seam = jnp.logical_or(low_seam, high_seam)
     has_low = jnp.logical_and(space > 0, jnp.logical_not(low_seam))
     has_high = jnp.logical_and(space < spaces - 1, jnp.logical_not(high_seam))
-    across = jnp.where(low_seam, space - 1, space + 1)
+    seams = ((high_seam, 0, 1), (low_seam, 1, -1))
     sibling_mode = high * 2 + (1 - core)
     sibling = (sibling_mode, space)
     partner = ((1 - high) * 2 + core, space)
     diagonal = ((1 - high) * 2 + (1 - core), space)
+    facing = (mode, sibling_mode, partner[0], diagonal[0])
     width = modes.shape[3]
     groups = [list(range(LATE))[i : i + 4] for i in range(0, LATE, 4)]
     planes = (3 * core, 1 + core, 2 - core, 3 - 3 * core)
@@ -134,7 +135,7 @@
 
     @pl.when(low_seam)
     def _():
-        for who in range(4):
+        for who in facing:
             signal((who, space - 1))
 
     loads = []
@@ -191,26 +192,24 @@
             device_id=(who, space + (1 if side == 0 else -1)), device_id_type=MESH,
         )
 
-    seam_side = jnp.where(low_seam, 1, 0)
-
-    def seam_copy(chip, other, source):
-        who = chip * 2 + (core if other == 0 else 1 - core)
-        return pltpu.make_async_remote_copy(
-            es.at[seam_side, other], sh.at[source], seam_s.at[chip, other], seam_r.at[source],
-            device_id=(who, across), device_id_type=MESH,
-        )
-
-    def pair_copy(other, source):
-        return pltpu.make_async_remote_copy(
-            es.at[seam_side, other], se.at[source], pair_s.at[other], pair_r.at[source],
+    def seam_copy(side, step, n, source):
+        return pltpu.make_async_remote_copy(
+            es.at[side, n % 2], sh.at[source], seam_s.at[n], seam_r.at[source],
+            device_id=(facing[n], space + step), device_id_type=MESH,
+        )
+
+    def pair_copy(side, other, source):
+        return pltpu.make_async_remote_copy(
+            es.at[side, other], se.at[source], pair_s.at[other], pair_r.at[source],
             device_id=partner if other == 0 else diagonal, device_id_type=MESH,
         )
 
     @pl.when(high_seam)
     def _():
-        for chip in range(2):
-            for other in range(2):
-                seam_copy(chip, other, mode).start()
+        for who in facing:
+            pl.semaphore_signal(ready, inc=1, device_id=(who, space + 1), device_id_type=MESH)
+        for n in range(4):
+            seam_copy(0, 1, n, mode).start()
 
     for there, side in ups:
         @pl.when(there)
@@ -218,10 +217,11 @@
             for other in range(2):
                 edge_copy(side, other, core).start()
 
-    @pl.when(seam)
-    def _():
-        for other in range(2):
-            pair_copy(other, core).start()
+    for there, side, _ in seams:
+        @pl.when(there)
+        def _():
+            for other in range(2):
+                pair_copy(side, other, core).start()
 
     for there, side in downs:
         @pl.when(jnp.logical_not(there))
@@ -506,29 +506,31 @@
         plane_copy(LATE + n).start()
         outer_copy(n).start()
 
+    for there, side, step in seams:
+        @pl.when(there)
+        def _():
+            for source in range(4):
+                seam_copy(side, step, 0, source).wait_recv()
+            for source in range(2):
+                pair_copy(side, 0, source).wait_recv()
+
+    @pl.when(low_seam)
+    def _():
+        pl.semaphore_wait(ready, 4)
+        for n in range(4):
+            seam_copy(1, -1, n, mode).start()
+
     @pl.when(seam)
     def _():
-        for source in range(4):
-            seam_copy(0, 0, source).wait_recv()
-
-        @pl.when(low_seam)
-        def _():
-            for chip in range(2):
-                for other in range(2):
-                    seam_copy(chip, other, mode).start()
-
-        for source in range(2):
-            pair_copy(0, source).wait_recv()
-
         def rows(ref, lead, r):
             return jnp.where(outer, ref[lead, pl.ds(r, 1), :], ref[lead, pl.ds(r + 1, 1), :])
 
-        facing = jnp.logical_or(
+        beside = jnp.logical_or(
             jnp.logical_and(low_seam, upper), jnp.logical_and(high_seam, jnp.logical_or(row == 7, row == 3))
         )
         for k in range(TERMS):
             faces = own_edges(c[k, 0], c[k, 1]) + rows(sh, high * 2 + k // 2, 10 + (k % 2) * 2)
-            gs[k] = jnp.where(facing, 0.5 * faces, 0.0)
+            gs[k] = jnp.where(beside, 0.5 * faces, 0.0)
         for b in range(CHIP):
             source = high * 2 + (core if b < GROUP else 1 - core)
             ds[b] = own_edges(m[b, 0], m[b, 1]) - rows(sh, source, (b % GROUP) * 2)
@@ -597,12 +599,13 @@
             for g in range(len(groups)):
                 edge_on(side, g).wait_send()
 
-    @pl.when(seam)
-    def _():
-        for other in range(2):
-            pair_copy(other, core).wait_send()
-            for chip in range(2):
-                seam_copy(chip, other, mode).wait_send()
+    for there, side, step in seams:
+        @pl.when(there)
+        def _():
+            for other in range(2):
+                pair_copy(side, other, core).wait_send()
+            for n in range(4):
+                seam_copy(side, step, n, mode).wait_send()
 
     for j in range(EVENS):
         item_copy(j).wait_send()
@@ -660,8 +663,8 @@
         pltpu.SMEM((24, 128), f32),
         dma((2, 4)), dma((3,)), dma((2,)), dma((3,)), dma((3,)), dma((2, 2)), dma((2, 2)), dma((EVENS,)), dma((EVENS,)),
         dma(()), dma(()), dma((EVENS,)), dma((EVENS,)),
-        dma((2, groups)), dma((2, groups)), dma((2, 2)), dma((4,)), dma((2,)), dma((2,)), dma((ENDS,)), dma((ENDS,)),
-        dma((3,)), dma((3,)),
+        dma((2, groups)), dma((2, groups)), dma((4,)), dma((4,)), dma((2,)), dma((2,)), dma((ENDS,)), dma((ENDS,)),
+        dma((3,)), dma((3,)), pltpu.SemaphoreType.REGULAR,
     ]
     anywhere = pl.BlockSpec(memory_space=pltpu.HBM)
     return pl.pallas_call(

time: 39.2 us -> 31.1 us (0.79)
  the two profiles are of different devices: /device:TPU:9 before, /device:TPU:1 now
where the time goes in v3:
time: 31.1 us; the launch traced here: 30.9 us
  Pallas kernels  30.1 us (97%)
  local copies, waits for them, and re-layouts  0.84 us (3%)
    pallas_call x1, Pallas kernels, galerkin(): pl.pallas_call(functools.partial(kernel, spaces), out_shape=jax.ShapeDtyp...  30.1 us
    unnamed x1, local copies, waits for them, and re-layouts  0.84 us

profile of v3, /device:TPU:1, one launch (start us, length us, event | category | flops | bytes accessed | tf_op | source)
XLA Modules:
  0.0 30.9 jit_solution(17819590920463551193)
XLA Ops:
  0.0 30.1 %galerkin.1 = f32[5,4,8,1024]{3,2,1,0:T(8,128)S(1)} custom-call(f32[5,4,8,1024]{3,2,1,0:T(8,128)} %modes.1, f32[4,4,8,1024]{3,2,1,0:T(8,128)} %coefs.1, s32[3,80]{1,0:T(4,128)} %bitcast.3, f32[1,80]{1,0:T(1,128)} %bitcast.4, s32[1,20]{1,0:T(1,128)} %bitcast.5), custom_call_target="tpu_custom_call" | custom-call | tf_op jit(solution)/shard_map/galerkin/pallas_call | solution.py:670
  30.1 0.8 %copy.7 = f32[5,4,8,1024]{3,2,1,0:T(8,128)} copy(f32[5,4,8,1024]{3,2,1,0:T(8,128)S(1)} %galerkin.1) | data formatting | bytes 1310720

commit v4 on v3

--- a/solution.py
+++ b/solution.py
@@ -14,8 +14,9 @@
 CHIP = 10
 TERMS = 4
 ENTRIES = 80
-EARLY = 2
-LATE = EVENS - 2
+EARLY = 4
+LATE = EARLY
+FIRST = 2
 ENDS = EVENS - LATE
 INF = 1 << 24
 
@@ -91,7 +92,7 @@
     spaces,
     modes, coefs, coupling, values, assignment, out,
     m, c, es, er, gy, gx, gz, db, gh, ak, dh, sb, rb, ts, tr, hs, hr, dr, akr, acc, sh, se, ds, gs,
-    rl, akl, drl, ghf, trf, drf, far,
+    rl, akl, drl, ghf, trf, drf, far, sp, sq,
     cv, vv, av, tiv, tfv, ti, tf,
     load_sem, small_sem, table_sem, sib_s, sib_r, edge_s, edge_r, item_s, item_r, tile_s, tile_r, plane_s, plane_r,
     fwd_s, fwd_r, seam_s, seam_r, pair_s, pair_r, outer_s, outer_r, give_s, give_r, ready,
@@ -113,7 +114,6 @@
     width = modes.shape[3]
     groups = [list(range(LATE))[i : i + 4] for i in range(0, LATE, 4)]
     planes = (3 * core, 1 + core, 2 - core, 3 - 3 * core)
-    theirs = (3 - 3 * core, 2 - core, 1 + core)
     ups = ((has_high, 0), (has_low, 1))
     downs = ((has_low, 0), (has_high, 1))
 
@@ -147,19 +147,6 @@
         for n, (source, target) in enumerate(((coupling, cv), (values, vv), (assignment, av)))
     ]
     for copy in smalls + loads:
-        copy.start()
-
-    peers = 2 + 2 * has_low.astype(i32) + 2 * has_high.astype(i32) + seam.astype(i32) + 4 * high_seam.astype(i32)
-    pl.semaphore_wait(barrier, peers)
-
-    to_sibling = [
-        pltpu.make_async_remote_copy(
-            modes.at[:, pl.ds(plane, 1)], m.at[pl.ds(GROUP, GROUP), pl.ds(at, 1)],
-            sib_s.at[at], sib_r.at[at], device_id=sibling, device_id_type=MESH,
-        )
-        for at, plane in enumerate(theirs)
-    ]
-    for copy in to_sibling:
         copy.start()
 
     for copy in smalls:
@@ -174,8 +161,21 @@
     for copy in table_copies:
         copy.start()
 
+    peers = 2 + 2 * has_low.astype(i32) + 2 * has_high.astype(i32) + seam.astype(i32) + 4 * high_seam.astype(i32)
+    pl.semaphore_wait(barrier, peers)
+
     for copy in loads:
         copy.wait()
+
+    to_sibling = [
+        pltpu.make_async_remote_copy(
+            m.at[pl.ds(0, GROUP), pl.ds(3 - at, 1)], m.at[pl.ds(GROUP, GROUP), pl.ds(at, 1)],
+            sib_s.at[at], sib_r.at[at], device_id=sibling, device_id_type=MESH,
+        )
+        for at in range(3)
+    ]
+    for copy in to_sibling:
+        copy.start()
 
     for side, row in ((0, 7), (1, 0)):
         for other, held in ((0, (0, 1)), (1, (3, 2))):
@@ -335,11 +335,14 @@
             stencil(mixed, (k,), store)
         sb[j, 0], sb[j, 1] = totals
 
-    for j in range(EARLY):
+    for j in range(FIRST):
         early_item(j)
         item_copy(j).start()
 
     lax.fori_loop(0, CHIP, own_stencil, 0)
+    for j in range(FIRST, EARLY):
+        begin_item(j, 0)
+        item_copy(j).start()
     lax.fori_loop(EARLY, EVENS, begin_item, 0)
 
     for there, side in downs:
@@ -375,14 +378,18 @@
         sb[j, 0] = sb[j, 0] + edge0
         sb[j, 1] = sb[j, 1] + edge1
         item_copy(j).start()
-        if j == LATE - 1:
-            pair = []
-            for n in range(EARLY):
-                slot, _, ours = item_of(n)
-                _, place, late_ours = item_of(LATE + n)
-                pair.append(edge_sum(slot, 0, 1.0 - ours, dh, gh, late_ours * dh[place]))
-            moved = jnp.where(jnp.logical_or(row == 1, row == 5), pltpu.roll(pair[1], 1, 0), pltpu.roll(pair[1], 7, 0))
-            ts[...] = jnp.where(jnp.logical_or(outer, middle), pair[0], moved)
+        if j == EARLY:
+            for t in range(2):
+                pair = []
+                for n in (2 * t, 2 * t + 1):
+                    slot, _, ours = item_of(n)
+                    packed = edge_sum(slot, 0, 1.0 - ours, dh, gh, None)
+                    if LATE + n < EVENS:
+                        _, place, ours = item_of(LATE + n)
+                        packed = packed + ours * dh[place]
+                    pair.append(packed)
+                moved = jnp.where(jnp.logical_or(row == 1, row == 5), pltpu.roll(pair[1], 1, 0), pltpu.roll(pair[1], 7, 0))
+                ts[t] = jnp.where(jnp.logical_or(outer, middle), pair[0], moved)
             tile_copy.start()
 
     def give(n, source, target):
@@ -442,6 +449,12 @@
             @pl.when(there)
             def _():
                 edge_on(side, g).start()
+        @pl.when(low_seam)
+        def _():
+            pl.semaphore_wait(ready, 4)
+            for n in range(4):
+                seam_copy(1, -1, n, mode).start()
+
         for j in members:
             plane_copy(j).wait_recv()
         lax.fori_loop(members[0], members[-1] + 1, raw_stencil, 0)
@@ -464,8 +477,9 @@
     lax.fori_loop(0, CHIP, remote_sum, 0)
 
     def unpack(ref, target):
-        target[0] = ref[...]
-        target[1] = jnp.where(upper, pltpu.roll(ref[...], 7, 0), pltpu.roll(ref[...], 1, 0))
+        for t in range(2):
+            target[2 * t] = ref[t]
+            target[2 * t + 1] = jnp.where(upper, pltpu.roll(ref[t], 7, 0), pltpu.roll(ref[t], 1, 0))
 
     tile_copy.wait_recv()
     tile_on.start()
@@ -497,31 +511,12 @@
 
     lax.fori_loop(0, CHIP, remote_edges, 0)
 
-    @pl.when(jnp.logical_not(seam))
-    def _():
-        sums_copy.start()
-
-    for n in range(ENDS):
-        item_copy(LATE + n).wait_recv()
-        plane_copy(LATE + n).start()
-        outer_copy(n).start()
-
-    for there, side, step in seams:
-        @pl.when(there)
-        def _():
-            for source in range(4):
-                seam_copy(side, step, 0, source).wait_recv()
-            for source in range(2):
-                pair_copy(side, 0, source).wait_recv()
-
-    @pl.when(low_seam)
-    def _():
-        pl.semaphore_wait(ready, 4)
-        for n in range(4):
-            seam_copy(1, -1, n, mode).start()
-
-    @pl.when(seam)
-    def _():
+    def seam_tiles(side, step):
+        for source in range(4):
+            seam_copy(side, step, 0, source).wait_recv()
+        for source in range(2):
+            pair_copy(side, 0, source).wait_recv()
+
         def rows(ref, lead, r):
             return jnp.where(outer, ref[lead, pl.ds(r, 1), :], ref[lead, pl.ds(r + 1, 1), :])
 
@@ -536,15 +531,28 @@
             ds[b] = own_edges(m[b, 0], m[b, 1]) - rows(sh, source, (b % GROUP) * 2)
             ds[CHIP + b] = rows(se, b // GROUP, (b % GROUP) * 2) - rows(sh, (1 - high) * 2 + b // GROUP, (b % GROUP) * 2)
 
-        def seam_sum(b, carry):
-            slot = slot_at(b)
-            edge0, edge1 = spread(edge_sum(slot, 16, 1.0, ds, gs, gs[0] * (tf[13, slot] * ds[b])))
+    def seam_sum(b):
+        slot = slot_at(b)
+        return edge_sum(slot, 16, 1.0, ds, gs, gs[0] * (tf[13, slot] * ds[b]))
+
+    @pl.when(high_seam)
+    def _():
+        seam_tiles(0, 1)
+
+        def seam_here(b, carry):
+            edge0, edge1 = spread(seam_sum(b))
             acc[b, 0] = acc[b, 0] + edge0
             acc[b, 1] = acc[b, 1] + edge1
             return carry
 
-        lax.fori_loop(0, CHIP, seam_sum, 0)
-        sums_copy.start()
+        lax.fori_loop(0, CHIP, seam_here, 0)
+
+    sums_copy.start()
+
+    for n in range(ENDS):
+        item_copy(LATE + n).wait_recv()
+        plane_copy(LATE + n).start()
+        outer_copy(n).start()
 
     def late_stencil(far_side, n):
         def store(k, p, value):
@@ -570,10 +578,10 @@
         at = jnp.maximum(index - LATE, 0)
         totals = [acc[b, 0], acc[b, 1], far[b, 1], far[b, 0]]
         totals = [total + weight * rl[at, p] for p, total in enumerate(totals)]
-        near_edge, far_edge = 0.0, 0.0
+        weight = jnp.where(index < EARLY, tf[12, slot], 0.0)
+        at = jnp.minimum(index, EARLY - 1)
+        near_edge, far_edge = weight * drl[at], weight * drf[at]
         for n in range(ENDS):
-            weight = jnp.where(index == n, tf[12, slot], 0.0)
-            near_edge, far_edge = near_edge + weight * drl[n], far_edge + weight * drf[n]
             weight, term = jnp.float32(0.0), jnp.int32(0)
             for cell in range(6):
                 found = ti[6 + cell, slot] == LATE + n
@@ -588,6 +596,31 @@
         return carry
 
     lax.fori_loop(0, GROUP, late_sum, 0)
+
+    @pl.when(low_seam)
+    def _():
+        seam_tiles(1, -1)
+
+        def seam_for_sibling(b, carry):
+            sp[b] = seam_sum(b + GROUP)
+            return carry
+
+        def seam_for_self(b, carry):
+            for plane, edge in zip(planes, spread(seam_sum(b))):
+                out[b, plane] = out[b, plane] + edge
+            return carry
+
+        def seam_from_sibling(b, carry):
+            for plane, edge in zip(planes[::-1], spread(sq[b])):
+                out[b, plane] = out[b, plane] + edge
+            return carry
+
+        lax.fori_loop(0, GROUP, seam_for_sibling, 0)
+        seam_give = give(3, sp, sq)
+        seam_give.start()
+        lax.fori_loop(0, GROUP, seam_for_self, 0)
+        seam_give.wait()
+        lax.fori_loop(0, GROUP, seam_from_sibling, 0)
 
     for copy in to_sibling:
         copy.wait_send()
@@ -636,8 +669,8 @@
         vmem((CHIP, 8, width), f32),
         vmem((EVENS, 2, 8, width), f32),
         vmem((LATE, 3, 8, width), f32),
-        vmem((8, width), f32),
-        vmem((8, width), f32),
+        vmem((2, 8, width), f32),
+        vmem((2, 8, width), f32),
         vmem((2, groups, 8, width), f32),
         vmem((2, groups, 8, width), f32),
         vmem((LATE, 8, width), f32),
@@ -649,11 +682,13 @@
         vmem((TERMS, 8, width), f32),
         vmem((ENDS, 4, 8, width), f32),
         vmem((ENDS * 3, 4, 8, width), f32),
-        vmem((ENDS, 8, width), f32),
+        vmem((EARLY, 8, width), f32),
         vmem((TERMS, 8, width), f32),
-        vmem((8, width), f32),
-        vmem((ENDS, 8, width), f32),
+        vmem((2, 8, width), f32),
+        vmem((EARLY, 8, width), f32),
         vmem((GROUP, 2, 8, width), f32),
+        vmem((GROUP, 8, width), f32),
+        vmem((GROUP, 8, width), f32),
         vmem(coupling.shape, jnp.int32),
         vmem(values.shape, f32),
         vmem(assignment.shape, jnp.int32),
@@ -664,7 +699,7 @@
         dma((2, 4)), dma((3,)), dma((2,)), dma((3,)), dma((3,)), dma((2, 2)), dma((2, 2)), dma((EVENS,)), dma((EVENS,)),
         dma(()), dma(()), dma((EVENS,)), dma((EVENS,)),
         dma((2, groups)), dma((2, groups)), dma((4,)), dma((4,)), dma((2,)), dma((2,)), dma((ENDS,)), dma((ENDS,)),
-        dma((3,)), dma((3,)), pltpu.SemaphoreType.REGULAR,
+        dma((4,)), dma((4,)), pltpu.SemaphoreType.REGULAR,
     ]
     anywhere = pl.BlockSpec(memory_space=pltpu.HBM)
     return pl.pallas_call(

time: 31.1 us -> 30.5 us (0.981)
  Pallas kernels: 30.1 us -> 29.5 us
    pallas_call x1, Pallas kernels: 30.1 us -> 29.5 us  [galerkin(): pl.pallas_call(functools.partial(kernel, spaces), out_shape=jax.ShapeDtyp...]
where the time goes in v4:
time: 30.5 us; the launch traced here: 30.4 us
  Pallas kernels  29.5 us (97%)
  local copies, waits for them, and re-layouts  0.84 us (3%)
    pallas_call x1, Pallas kernels, galerkin(): pl.pallas_call(functools.partial(kernel, spaces), out_shape=jax.ShapeDtyp...  29.5 us
    unnamed x1, local copies, waits for them, and re-layouts  0.84 us

profile of v4, /device:TPU:1, one launch (start us, length us, event | category | flops | bytes accessed | tf_op | source)
XLA Modules:
  0.0 30.4 jit_solution(13012828561676449173)
XLA Ops:
  0.0 29.5 %galerkin.1 = f32[5,4,8,1024]{3,2,1,0:T(8,128)S(1)} custom-call(f32[5,4,8,1024]{3,2,1,0:T(8,128)} %modes.1, f32[4,4,8,1024]{3,2,1,0:T(8,128)} %coefs.1, s32[3,80]{1,0:T(4,128)} %bitcast.3, f32[1,80]{1,0:T(1,128)} %bitcast.4, s32[1,20]{1,0:T(1,128)} %bitcast.5), custom_call_target="tpu_custom_call" | custom-call | tf_op jit(solution)/shard_map/galerkin/pallas_call | solution.py:705
  29.6 0.8 %copy.7 = f32[5,4,8,1024]{3,2,1,0:T(8,128)} copy(f32[5,4,8,1024]{3,2,1,0:T(8,128)S(1)} %galerkin.1) | data formatting | bytes 1310720

commit v5 on v4

--- a/solution.py
+++ b/solution.py
@@ -14,9 +14,8 @@
 CHIP = 10
 TERMS = 4
 ENTRIES = 80
-EARLY = 4
-LATE = EARLY
-FIRST = 2
+EARLY = 3
+LATE = 4
 ENDS = EVENS - LATE
 INF = 1 << 24
 
@@ -335,14 +334,11 @@
             stencil(mixed, (k,), store)
         sb[j, 0], sb[j, 1] = totals
 
-    for j in range(FIRST):
+    for j in range(EARLY):
         early_item(j)
         item_copy(j).start()
 
     lax.fori_loop(0, CHIP, own_stencil, 0)
-    for j in range(FIRST, EARLY):
-        begin_item(j, 0)
-        item_copy(j).start()
     lax.fori_loop(EARLY, EVENS, begin_item, 0)
 
     for there, side in downs:
@@ -370,6 +366,16 @@
         source = core if b < GROUP else 1 - core
         dh[b] = own_edges(m[b, 0], m[b, 1]) - tile(*arrived(er, (source,), (b % GROUP) * 2))
 
+    def merged(one, two):
+        which = lax.broadcasted_iota(i32, one.shape, 0)
+        stay = (which % 4 == 0) | (which % 4 == 3)
+        moved = jnp.where(which % 4 == 1, pltpu.roll(two, 1, 0), pltpu.roll(two, 7, 0))
+        return jnp.where(stay, one, moved)
+
+    def second(both):
+        which = lax.broadcasted_iota(i32, both.shape, 0)
+        return jnp.where(which % 4 == 0, pltpu.roll(both, 7, 0), pltpu.roll(both, 1, 0))
+
     tile_copy = pltpu.make_async_remote_copy(ts, tr, tile_s, tile_r, device_id=partner, device_id_type=MESH)
 
     for j in range(EARLY, EVENS):
@@ -379,17 +385,14 @@
         sb[j, 1] = sb[j, 1] + edge1
         item_copy(j).start()
         if j == EARLY:
-            for t in range(2):
-                pair = []
-                for n in (2 * t, 2 * t + 1):
-                    slot, _, ours = item_of(n)
-                    packed = edge_sum(slot, 0, 1.0 - ours, dh, gh, None)
-                    if LATE + n < EVENS:
-                        _, place, ours = item_of(LATE + n)
-                        packed = packed + ours * dh[place]
-                    pair.append(packed)
-                moved = jnp.where(jnp.logical_or(row == 1, row == 5), pltpu.roll(pair[1], 1, 0), pltpu.roll(pair[1], 7, 0))
-                ts[t] = jnp.where(jnp.logical_or(outer, middle), pair[0], moved)
+            parts = []
+            for n in range(EARLY):
+                slot, _, ours = item_of(n)
+                packed = edge_sum(slot, 0, 1.0 - ours, dh, gh, None)
+                _, place, ours = item_of(LATE + n)
+                parts.append(packed + ours * dh[place])
+            ts[:, pl.ds(0, width)] = merged(parts[0], parts[1])
+            ts[:, pl.ds(width, width // 2)] = merged(parts[2][:, : width // 2], parts[2][:, width // 2 :])
             tile_copy.start()
 
     def give(n, source, target):
@@ -477,9 +480,10 @@
     lax.fori_loop(0, CHIP, remote_sum, 0)
 
     def unpack(ref, target):
-        for t in range(2):
-            target[2 * t] = ref[t]
-            target[2 * t + 1] = jnp.where(upper, pltpu.roll(ref[t], 7, 0), pltpu.roll(ref[t], 1, 0))
+        target[0] = ref[:, pl.ds(0, width)]
+        target[1] = second(ref[:, pl.ds(0, width)])
+        target[2, :, pl.ds(0, width // 2)] = ref[:, pl.ds(width, width // 2)]
+        target[2, :, pl.ds(width // 2, width // 2)] = second(ref[:, pl.ds(width, width // 2)])
 
     tile_copy.wait_recv()
     tile_on.start()
@@ -669,8 +673,8 @@
         vmem((CHIP, 8, width), f32),
         vmem((EVENS, 2, 8, width), f32),
         vmem((LATE, 3, 8, width), f32),
-        vmem((2, 8, width), f32),
-        vmem((2, 8, width), f32),
+        vmem((8, width + width // 2), f32),
+        vmem((8, width + width // 2), f32),
         vmem((2, groups, 8, width), f32),
         vmem((2, groups, 8, width), f32),
         vmem((LATE, 8, width), f32),
@@ -684,7 +688,7 @@
         vmem((ENDS * 3, 4, 8, width), f32),
         vmem((EARLY, 8, width), f32),
         vmem((TERMS, 8, width), f32),
-        vmem((2, 8, width), f32),
+        vmem((8, width + width // 2), f32),
         vmem((EARLY, 8, width), f32),
         vmem((GROUP, 2, 8, width), f32),
         vmem((GROUP, 8, width), f32),

time: 30.5 us -> 29.9 us (0.980)
  Pallas kernels: 29.5 us -> 28.9 us
    pallas_call x1, Pallas kernels: 29.5 us -> 28.9 us  [galerkin(): pl.pallas_call(functools.partial(kernel, spaces), out_shape=jax.ShapeDtyp...]
where the time goes in v5:
time: 29.9 us; the launch traced here: 29.8 us
  Pallas kernels  28.9 us (97%)
  local copies, waits for them, and re-layouts  0.84 us (3%)
    pallas_call x1, Pallas kernels, galerkin(): pl.pallas_call(functools.partial(kernel, spaces), out_shape=jax.ShapeDtyp...  28.9 us
    unnamed x1, local copies, waits for them, and re-layouts  0.84 us

profile of v5, /device:TPU:1, one launch (start us, length us, event | category | flops | bytes accessed | tf_op | source)
XLA Modules:
  0.0 29.8 jit_solution(641861464481484588)
XLA Ops:
  0.0 28.9 %galerkin.1 = f32[5,4,8,1024]{3,2,1,0:T(8,128)S(1)} custom-call(f32[5,4,8,1024]{3,2,1,0:T(8,128)} %modes.1, f32[4,4,8,1024]{3,2,1,0:T(8,128)} %coefs.1, s32[3,80]{1,0:T(4,128)} %bitcast.3, f32[1,80]{1,0:T(1,128)} %bitcast.4, s32[1,20]{1,0:T(1,128)} %bitcast.5), custom_call_target="tpu_custom_call" | custom-call | tf_op jit(solution)/shard_map/galerkin/pallas_call | solution.py:709
  28.9 0.8 %copy.7 = f32[5,4,8,1024]{3,2,1,0:T(8,128)} copy(f32[5,4,8,1024]{3,2,1,0:T(8,128)S(1)} %galerkin.1) | data formatting | bytes 1310720

commit v6 on v5

--- a/solution.py
+++ b/solution.py
@@ -94,7 +94,7 @@
     rl, akl, drl, ghf, trf, drf, far, sp, sq,
     cv, vv, av, tiv, tfv, ti, tf,
     load_sem, small_sem, table_sem, sib_s, sib_r, edge_s, edge_r, item_s, item_r, tile_s, tile_r, plane_s, plane_r,
-    fwd_s, fwd_r, seam_s, seam_r, pair_s, pair_r, outer_s, outer_r, give_s, give_r, ready,
+    fwd_s, fwd_r, seam_s, seam_r, pair_s, pair_r, outer_s, outer_r, give_s, give_r, ready, inner_s, inner_r,
 ):
     f32, i32 = jnp.float32, jnp.int32
     mode, space = lax.axis_index("mode"), lax.axis_index("space")
@@ -304,9 +304,17 @@
         return packed
 
     def item_copy(j):
-        target = rb.at[j, pl.ds(0, 2)] if j < LATE else rl.at[j - LATE, pl.ds(0, 2)]
-        return pltpu.make_async_remote_copy(
-            sb.at[j], target, item_s.at[j], item_r.at[j], device_id=partner, device_id_type=MESH
+        source, target = sb.at[j], rb.at[j, pl.ds(0, 2)] if j < LATE else rl.at[j - LATE, pl.ds(0, 1)]
+        if j >= LATE:
+            source = sb.at[j, pl.ds(0, 1)]
+        return pltpu.make_async_remote_copy(
+            source, target, item_s.at[j], item_r.at[j], device_id=partner, device_id_type=MESH
+        )
+
+    def inner_copy(n):
+        return pltpu.make_async_remote_copy(
+            sb.at[LATE + n, pl.ds(1, 1)], rl.at[n, pl.ds(1, 1)], inner_s.at[n], inner_r.at[n],
+            device_id=partner, device_id_type=MESH,
         )
 
     def item_of(j):
@@ -383,6 +391,8 @@
         edge0, edge1 = spread(edge_sum(slot, 0, 1.0 - ours, dh, gh, None))
         sb[j, 0] = sb[j, 0] + edge0
         sb[j, 1] = sb[j, 1] + edge1
+        if j >= LATE:
+            inner_copy(j - LATE).start()
         item_copy(j).start()
         if j == EARLY:
             parts = []
@@ -554,8 +564,9 @@
     sums_copy.start()
 
     for n in range(ENDS):
+        inner_copy(n).wait_recv()
+        plane_copy(LATE + n).start()
         item_copy(LATE + n).wait_recv()
-        plane_copy(LATE + n).start()
         outer_copy(n).start()
 
     def late_stencil(far_side, n):
@@ -649,6 +660,7 @@
         plane_copy(j).wait_send()
     for n in range(ENDS):
         outer_copy(n).wait_send()
+        inner_copy(n).wait_send()
     for copy in (tile_copy, faces_copy, tile_on, sums_copy):
         copy.wait_send()
 
@@ -703,7 +715,7 @@
         dma((2, 4)), dma((3,)), dma((2,)), dma((3,)), dma((3,)), dma((2, 2)), dma((2, 2)), dma((EVENS,)), dma((EVENS,)),
         dma(()), dma(()), dma((EVENS,)), dma((EVENS,)),
         dma((2, groups)), dma((2, groups)), dma((4,)), dma((4,)), dma((2,)), dma((2,)), dma((ENDS,)), dma((ENDS,)),
-        dma((4,)), dma((4,)), pltpu.SemaphoreType.REGULAR,
+        dma((4,)), dma((4,)), pltpu.SemaphoreType.REGULAR, dma((ENDS,)), dma((ENDS,)),
     ]
     anywhere = pl.BlockSpec(memory_space=pltpu.HBM)
     return pl.pallas_call(

time: 29.9 us -> 30 us (level)
  no operation moved by 1% of the time
where the time goes in v6:
time: 30 us; the launch traced here: 29.8 us
  Pallas kernels  29 us (97%)
  local copies, waits for them, and re-layouts  0.84 us (3%)
    pallas_call x1, Pallas kernels, galerkin(): pl.pallas_call(functools.partial(kernel, spaces), out_shape=jax.ShapeDtyp...  29 us
    unnamed x1, local copies, waits for them, and re-layouts  0.84 us

profile of v6, /device:TPU:1, one launch (start us, length us, event | category | flops | bytes accessed | tf_op | source)
XLA Modules:
  0.0 29.8 jit_solution(9788154406125002788)
XLA Ops:
  0.0 29.0 %galerkin.1 = f32[5,4,8,1024]{3,2,1,0:T(8,128)S(1)} custom-call(f32[5,4,8,1024]{3,2,1,0:T(8,128)} %modes.1, f32[4,4,8,1024]{3,2,1,0:T(8,128)} %coefs.1, s32[3,80]{1,0:T(4,128)} %bitcast.3, f32[1,80]{1,0:T(1,128)} %bitcast.4, s32[1,20]{1,0:T(1,128)} %bitcast.5), custom_call_target="tpu_custom_call" | custom-call | tf_op jit(solution)/shard_map/galerkin/pallas_call | solution.py:721
  29.0 0.8 %copy.7 = f32[5,4,8,1024]{3,2,1,0:T(8,128)} copy(f32[5,4,8,1024]{3,2,1,0:T(8,128)S(1)} %galerkin.1) | data formatting | bytes 1310720
